TPU v7x, 32 devices: a whole 2x2x4 slice. The times are simulated.
32 devices in a mesh: dp: 4 (over y, core), ctx: 4 (over z), fsdp: 2 (over x).
Axes of the slice: x: 2, y: 2, z: 4, core: 2. Of those that a mesh axis runs over, the one named last changes fastest.
Arguments:
- tokens: bfloat16 [8, 1024, 2048], P(('dp', 'fsdp'), 'ctx'), may hold values from -6 to 6
- cotangent: bfloat16 [8, 1024, 2048], P(('dp', 'fsdp'), 'ctx'), may hold values from -6 to 6
- norm1_gain: float32 [2048], P('fsdp'), may hold values from 0.5 to 1.5
- norm1_bias: float32 [2048], P('fsdp'), may hold values from -1.5 to 1.5
- norm2_gain: float32 [2048], P('fsdp'), may hold values from 0.5 to 1.5
- norm2_bias: float32 [2048], P('fsdp'), may hold values from -1.5 to 1.5
- w_query: bfloat16 [2048, 2048], P('fsdp'), may hold values from -0.125 to 0.125
- w_key: bfloat16 [2048, 2048], P('fsdp'), may hold values from -0.125 to 0.125
- w_value: bfloat16 [2048, 2048], P('fsdp'), may hold values from -0.125 to 0.125
- b_query: float32 [2048], P('fsdp'), may hold values from -1.5 to 1.5
- b_key: float32 [512], P('fsdp'), may hold values from -1.5 to 1.5
- b_value: float32 [2048], P('fsdp'), may hold values from -1.5 to 1.5
- w_out: bfloat16 [2048, 2048], P('fsdp'), may hold values from -0.5 to 0.5
- b_out: float32 [2048], P('fsdp'), may hold values from -1.5 to 1.5
- w_up: bfloat16 [2048, 8192], P('fsdp'), may hold values from -0.125 to 0.125
- b_up: float32 [8192], P('fsdp'), may hold values from -1.5 to 1.5
- w_down: bfloat16 [2048, 8192], P('fsdp'), may hold values from -0.0625 to 0.0625
- b_down: float32 [2048], P('fsdp'), may hold values from -1.5 to 1.5
Outputs:
- mixed: bfloat16 [8, 1024, 2048], P(('dp', 'fsdp'), 'ctx')
- grad_tokens: float32 [8, 1024, 2048], P(('dp', 'fsdp'), 'ctx')
- grad_norm1_gain: float32 [2048], P('fsdp')
- grad_norm1_bias: float32 [2048], P('fsdp')
- grad_norm2_gain: float32 [2048], P('fsdp')
- grad_norm2_bias: float32 [2048], P('fsdp')
- grad_w_query: float32 [2048, 2048], P('fsdp')
- grad_w_key: float32 [2048, 2048], P('fsdp')
- grad_w_value: float32 [2048, 2048], P('fsdp')
- grad_b_query: float32 [2048], P('fsdp')
- grad_b_key: float32 [512], P('fsdp')
- grad_b_value: float32 [2048], P('fsdp')
- grad_w_out: float32 [2048, 2048], P('fsdp')
- grad_b_out: float32 [2048], P('fsdp')
- grad_w_up: float32 [2048, 8192], P('fsdp')
- grad_b_up: float32 [8192], P('fsdp')
- grad_w_down: float32 [2048, 8192], P('fsdp')
- grad_b_down: float32 [2048], P('fsdp')
All inputs are finite; a program needn't handle non-finite values.
Results may differ from a plain program's by a relative error of at most 0.025.
Values may be sent and summed in bfloat16 or wider, within the bound.
No kernel may reach another device: no remote copies, remote signals or barrier semaphores. Data moves between devices by JAX's collectives and lax.ppermute only.
A program may use at most 768 MiB of HBM per device.

v0:
```python
import math

import jax
import jax.numpy as jnp
from jax import lax
from jax.sharding import PartitionSpec as P

HEAD_DIM = 256
ROT = 64


norm_eps = 1e-05
masked_score = -1e30
contract_rows = (((1,), (1,)), ((), ()))
contract_tokens = (((0,), (0,)), ((), ()))


def layer_norm(values, gain_vec, shift_vec):
    center = values - jnp.mean(values, axis=-1, keepdims=True)
    spread = jnp.mean(center * center, axis=-1, keepdims=True)
    return center * lax.rsqrt(spread + norm_eps) * gain_vec + shift_vec


def exact_gelu(values):
    return jax.nn.gelu(values, approximate=False)


def angle_tables(position):
    half_rot = ROT // 2
    inverse = 10000.0 ** (-2.0 * jnp.arange(half_rot, dtype=jnp.float32) / ROT)
    angles = position.astype(jnp.float32)[:, None] * inverse[None, :]
    return (jnp.cos(angles), jnp.sin(angles))


def rotate(values, cosine, sine_part):
    half_rot = ROT // 2
    first_half = values[..., :half_rot]
    second_half = values[..., half_rot:ROT]
    cos_wide = cosine[:, None, :]
    sin_wide = sine_part[:, None, :]
    return jnp.concatenate(
        [
            first_half * cos_wide - second_half * sin_wide,
            second_half * cos_wide + first_half * sin_wide,
            values[..., ROT:],
        ],
        axis=-1,
    )


def rows_dot(left, right):
    return lax.dot_general(left, right, contract_rows, preferred_element_type=jnp.float32)


def token_dot(left, right):
    return lax.dot_general(left, right, contract_tokens, preferred_element_type=jnp.float32)


def local(
    tokens,
    cotangent,
    norm1_gain,
    norm1_bias,
    norm2_gain,
    norm2_bias,
    w_query,
    w_key,
    w_value,
    b_query,
    b_key,
    b_value,
    w_out,
    b_out,
    w_up,
    b_up,
    w_down,
    b_down,
):
    small_full = (
        lax.all_gather(norm1_gain, "fsdp", axis=0, tiled=True),
        lax.all_gather(norm1_bias, "fsdp", axis=0, tiled=True),
        lax.all_gather(norm2_gain, "fsdp", axis=0, tiled=True),
        lax.all_gather(norm2_bias, "fsdp", axis=0, tiled=True),
        lax.all_gather(b_query, "fsdp", axis=0, tiled=True),
        lax.all_gather(b_key, "fsdp", axis=0, tiled=True),
        lax.all_gather(b_value, "fsdp", axis=0, tiled=True),
        lax.all_gather(b_out, "fsdp", axis=0, tiled=True),
        lax.all_gather(b_up, "fsdp", axis=0, tiled=True),
        lax.all_gather(b_down, "fsdp", axis=0, tiled=True),
    )
    (
        gain_one,
        shift_one,
        gain_two,
        shift_two,
        query_shift,
        key_part,
        value_shift,
        out_shift,
        up_shift,
        down_shift,
    ) = small_full
    rows_in = tokens[0].astype(jnp.float32)
    local_rows = rows_in.shape[0]
    model_width = rows_in.shape[1]
    hidden_width = w_up.shape[1]
    head_count = model_width // HEAD_DIM
    scale_root = math.sqrt(HEAD_DIM)
    first_norm, pull_first = jax.vjp(layer_norm, rows_in, gain_one, shift_one)
    second_norm, pull_second = jax.vjp(layer_norm, rows_in, gain_two, shift_two)
    first_in = first_norm.astype(jnp.bfloat16)
    second_in = second_norm.astype(jnp.bfloat16)
    piece_q = lax.all_gather(w_query, "fsdp", axis=0, tiled=True)
    piece_k = lax.all_gather(w_key, "fsdp", axis=0, tiled=True)
    piece_v = lax.all_gather(w_value, "fsdp", axis=0, tiled=True)
    piece_u = lax.all_gather(w_up, "fsdp", axis=0, tiled=True)
    span_rows = piece_q.shape[0]
    query_acc = jnp.dot(first_in, piece_q, preferred_element_type=jnp.float32)
    key_acc = jnp.dot(first_in, piece_k, preferred_element_type=jnp.float32)
    value_acc = jnp.dot(first_in, piece_v, preferred_element_type=jnp.float32)
    up_acc = jnp.dot(second_in, piece_u, preferred_element_type=jnp.float32)
    key_shift = jnp.pad(key_part.reshape(head_count, ROT), ((0, 0), (0, HEAD_DIM - ROT))).reshape(
        model_width
    )
    ctx_start = lax.axis_index("ctx") * local_rows
    position = ctx_start + jnp.arange(local_rows, dtype=jnp.int32)
    cosine, sine_part = angle_tables(position)
    query_rot = rotate(
        (query_acc + query_shift).reshape(local_rows, head_count, HEAD_DIM), cosine, sine_part
    ).astype(jnp.bfloat16)
    key_rot = rotate(
        (key_acc + key_shift).reshape(local_rows, head_count, HEAD_DIM), cosine, sine_part
    ).astype(jnp.bfloat16)
    value_low = (value_acc + value_shift).astype(jnp.bfloat16)
    key_flat = key_rot.reshape(local_rows, model_width)
    hidden_pre = up_acc + up_shift
    last_query = ctx_start + local_rows - 1
    start_state = (
        jnp.full((head_count, local_rows), masked_score, jnp.float32),
        jnp.zeros((head_count, local_rows), jnp.float32),
        jnp.zeros((head_count, local_rows, HEAD_DIM), jnp.float32),
    )
    piece_k = lax.all_gather(key_flat, "ctx", axis=0, tiled=True)
    piece_v = lax.all_gather(value_low, "ctx", axis=0, tiled=True)
    span_rows = piece_k.shape[0]

    def attend_work(current):
        best_score, row_total, summed = current
        key_heads = piece_k.reshape(span_rows, head_count, HEAD_DIM)
        value_heads = piece_v.reshape(span_rows, head_count, HEAD_DIM)
        scores = (
            jnp.einsum("qhd,khd->hqk", query_rot, key_heads, preferred_element_type=jnp.float32)
            / scale_root
        )
        key_pos = jnp.arange(span_rows, dtype=jnp.int32)
        allowed = (key_pos[None, :] <= position[:, None])[None]
        higher = jnp.maximum(best_score, jnp.max(jnp.where(allowed, scores, masked_score), axis=-1))
        exp_terms = jnp.where(allowed, jnp.exp(scores - higher[..., None]), 0.0)
        added = jnp.einsum(
            "hqk,khd->hqd",
            exp_terms.astype(jnp.bfloat16),
            value_heads,
            preferred_element_type=jnp.float32,
        )
        return (higher, jnp.sum(exp_terms, axis=-1), added)

    def skip_work(current):
        return current

    best_score, row_total, summed = lax.cond(
        jnp.int32(0) <= last_query, attend_work, skip_work, start_state
    )
    attended = summed / row_total[..., None]
    log_total = best_score + jnp.log(row_total)
    attended_low = (
        jnp.transpose(attended, (1, 0, 2)).reshape(local_rows, model_width).astype(jnp.bfloat16)
    )
    activated = exact_gelu(hidden_pre).astype(jnp.bfloat16)
    piece_o, piece_d = lax.all_gather((w_out, w_down), "fsdp", axis=0, tiled=True)
    branch_sum = rows_dot(attended_low, piece_o) + rows_dot(activated, piece_d)
    mixed_out = (rows_in + branch_sum + out_shift + down_shift).astype(jnp.bfloat16)
    grad_out = cotangent[0]
    grad_rows = grad_out.astype(jnp.float32)
    piece_o = lax.all_gather(w_out, "fsdp", axis=0, tiled=True)
    piece_d = lax.all_gather(w_down, "fsdp", axis=0, tiled=True)
    grad_att = jnp.dot(grad_out, piece_o, preferred_element_type=jnp.float32)
    grad_act = jnp.dot(grad_out, piece_d, preferred_element_type=jnp.float32)
    gelu_value, gelu_pull = jax.vjp(exact_gelu, hidden_pre)
    grad_pre = gelu_pull(grad_act)[0].astype(jnp.bfloat16)
    grad_heads = grad_att.astype(jnp.bfloat16).reshape(local_rows, head_count, HEAD_DIM)
    key_all, value_all = (
        lax.all_gather(key_flat, "ctx", axis=0, tiled=True),
        lax.all_gather(value_low, "ctx", axis=0, tiled=True),
    )
    seq_len = key_all.shape[0]
    key_heads = key_all.reshape(seq_len, head_count, HEAD_DIM)
    value_heads = value_all.reshape(seq_len, head_count, HEAD_DIM)
    scores = (
        jnp.einsum("qhd,khd->hqk", query_rot, key_heads, preferred_element_type=jnp.float32)
        / scale_root
    )
    allowed = (jnp.arange(seq_len, dtype=jnp.int32)[None, :] <= position[:, None])[None]
    chance = jnp.where(allowed, jnp.exp(scores - log_total[..., None]), 0.0)
    grad_chance = jnp.einsum(
        "qhd,khd->hqk", grad_heads, value_heads, preferred_element_type=jnp.float32
    )
    row_dot = jnp.sum(jnp.transpose(grad_heads.astype(jnp.float32), (1, 0, 2)) * attended, axis=-1)
    grad_score = (chance * (grad_chance - row_dot[..., None])).astype(jnp.bfloat16)
    grad_qrot = (
        jnp.einsum("hqk,khd->qhd", grad_score, key_heads, preferred_element_type=jnp.float32)
        / scale_root
    )
    key_term = (
        jnp.einsum("hqk,qhd->khd", grad_score, query_rot, preferred_element_type=jnp.float32)
        / scale_root
    )
    value_term = jnp.einsum(
        "hqk,qhd->khd", chance.astype(jnp.bfloat16), grad_heads, preferred_element_type=jnp.float32
    )
    grad_krot, grad_vfull = (
        lax.psum_scatter(
            key_term.reshape(seq_len, model_width).astype(jnp.bfloat16),
            "ctx",
            scatter_dimension=0,
            tiled=True,
        ).astype(jnp.float32),
        lax.psum_scatter(
            value_term.reshape(seq_len, model_width).astype(jnp.bfloat16),
            "ctx",
            scatter_dimension=0,
            tiled=True,
        ).astype(jnp.float32),
    )
    grad_query = (
        rotate(grad_qrot, cosine, -sine_part).reshape(local_rows, model_width).astype(jnp.bfloat16)
    )
    grad_key = (
        rotate(grad_krot.reshape(local_rows, head_count, HEAD_DIM), cosine, -sine_part)
        .reshape(local_rows, model_width)
        .astype(jnp.bfloat16)
    )
    grad_value = grad_vfull.astype(jnp.bfloat16)
    piece_q, back_piece_k, back_piece_v, piece_u = lax.all_gather(
        (w_query, w_key, w_value, w_up), "fsdp", axis=0, tiled=True
    )
    first_sum = (
        rows_dot(grad_query, piece_q)
        + rows_dot(grad_key, back_piece_k)
        + rows_dot(grad_value, back_piece_v)
    )
    grad_norms = jnp.stack([first_sum, rows_dot(grad_pre, piece_u)])
    grad_in_one, grad_gain_one, grad_shift_one = pull_first(grad_norms[0])
    grad_in_two, grad_gain_two, grad_shift_two = pull_second(grad_norms[1])
    grad_tokens = (grad_rows + grad_in_one + grad_in_two)[None]
    key_bias_term = jnp.sum(
        grad_key.astype(jnp.float32).reshape(local_rows, head_count, HEAD_DIM)[..., :ROT], axis=0
    ).reshape(head_count * ROT)
    out_term = jnp.sum(grad_rows, axis=0)
    small_shards = (
        lax.psum_scatter(
            grad_gain_one.astype(jnp.bfloat16), "fsdp", scatter_dimension=0, tiled=True
        ).astype(jnp.float32),
        lax.psum_scatter(
            grad_shift_one.astype(jnp.bfloat16), "fsdp", scatter_dimension=0, tiled=True
        ).astype(jnp.float32),
        lax.psum_scatter(
            grad_gain_two.astype(jnp.bfloat16), "fsdp", scatter_dimension=0, tiled=True
        ).astype(jnp.float32),
        lax.psum_scatter(
            grad_shift_two.astype(jnp.bfloat16), "fsdp", scatter_dimension=0, tiled=True
        ).astype(jnp.float32),
        lax.psum_scatter(
            jnp.sum(grad_query.astype(jnp.float32), axis=0).astype(jnp.bfloat16),
            "fsdp",
            scatter_dimension=0,
            tiled=True,
        ).astype(jnp.float32),
        lax.psum_scatter(
            key_bias_term.astype(jnp.bfloat16), "fsdp", scatter_dimension=0, tiled=True
        ).astype(jnp.float32),
        lax.psum_scatter(
            jnp.sum(grad_value.astype(jnp.float32), axis=0).astype(jnp.bfloat16),
            "fsdp",
            scatter_dimension=0,
            tiled=True,
        ).astype(jnp.float32),
        lax.psum_scatter(
            out_term.astype(jnp.bfloat16), "fsdp", scatter_dimension=0, tiled=True
        ).astype(jnp.float32),
        lax.psum_scatter(
            jnp.sum(grad_pre.astype(jnp.float32), axis=0).astype(jnp.bfloat16),
            "fsdp",
            scatter_dimension=0,
            tiled=True,
        ).astype(jnp.float32),
        lax.psum_scatter(
            out_term.astype(jnp.bfloat16), "fsdp", scatter_dimension=0, tiled=True
        ).astype(jnp.float32),
    )
    right_one = jnp.concatenate([grad_query, grad_key, grad_value], axis=1)

    def term_maker(left_one, left_out, left_two):

        def grad_term(row_start, row_count):
            return jnp.concatenate(
                [
                    token_dot(left_one, right_one),
                    token_dot(left_out, attended_low),
                    token_dot(left_two, grad_pre),
                    token_dot(left_out, activated),
                ],
                axis=1,
            )

        return grad_term

    grad_term = term_maker(first_in, grad_out, second_in)
    fsdp_shard = lax.psum_scatter(
        grad_term(
            jnp.int32(0), lax.axis_size("fsdp") * (model_width // lax.axis_size("fsdp"))
        ).astype(jnp.bfloat16),
        "fsdp",
        scatter_dimension=0,
        tiled=True,
    )
    summed_all = (
        lax.psum(fsdp_shard, ("dp", "ctx")).astype(jnp.float32),
        lax.psum(small_shards[0].astype(jnp.bfloat16), ("dp", "ctx")).astype(jnp.float32),
        lax.psum(small_shards[1].astype(jnp.bfloat16), ("dp", "ctx")).astype(jnp.float32),
        lax.psum(small_shards[2].astype(jnp.bfloat16), ("dp", "ctx")).astype(jnp.float32),
        lax.psum(small_shards[3].astype(jnp.bfloat16), ("dp", "ctx")).astype(jnp.float32),
        lax.psum(small_shards[4].astype(jnp.bfloat16), ("dp", "ctx")).astype(jnp.float32),
        lax.psum(small_shards[5].astype(jnp.bfloat16), ("dp", "ctx")).astype(jnp.float32),
        lax.psum(small_shards[6].astype(jnp.bfloat16), ("dp", "ctx")).astype(jnp.float32),
        lax.psum(small_shards[7].astype(jnp.bfloat16), ("dp", "ctx")).astype(jnp.float32),
        lax.psum(small_shards[8].astype(jnp.bfloat16), ("dp", "ctx")).astype(jnp.float32),
        lax.psum(small_shards[9].astype(jnp.bfloat16), ("dp", "ctx")).astype(jnp.float32),
    )
    grad_shard = summed_all[0]
    small_sums = summed_all[1:]
    edge_out = 4 * model_width
    edge_up = edge_out + hidden_width
    return (
        mixed_out[None],
        grad_tokens,
        small_sums[0],
        small_sums[1],
        small_sums[2],
        small_sums[3],
        grad_shard[:, :model_width],
        grad_shard[:, model_width : 2 * model_width],
        grad_shard[:, 2 * model_width : 3 * model_width],
        small_sums[4],
        small_sums[5],
        small_sums[6],
        grad_shard[:, 3 * model_width : edge_out],
        small_sums[7],
        grad_shard[:, edge_out:edge_up],
        small_sums[8],
        grad_shard[:, edge_up:],
        small_sums[9],
    )


def solution(mesh):
    in_specs = (
        P(("dp", "fsdp"), "ctx", None),
        P(("dp", "fsdp"), "ctx", None),
        P("fsdp"),
        P("fsdp"),
        P("fsdp"),
        P("fsdp"),
        P("fsdp", None),
        P("fsdp", None),
        P("fsdp", None),
        P("fsdp"),
        P("fsdp"),
        P("fsdp"),
        P("fsdp", None),
        P("fsdp"),
        P("fsdp", None),
        P("fsdp"),
        P("fsdp", None),
        P("fsdp"),
    )
    out_specs = (
        P(("dp", "fsdp"), "ctx", None),
        P(("dp", "fsdp"), "ctx", None),
        P("fsdp"),
        P("fsdp"),
        P("fsdp"),
        P("fsdp"),
        P("fsdp", None),
        P("fsdp", None),
        P("fsdp", None),
        P("fsdp"),
        P("fsdp"),
        P("fsdp"),
        P("fsdp", None),
        P("fsdp"),
        P("fsdp", None),
        P("fsdp"),
        P("fsdp", None),
        P("fsdp"),
    )
    return jax.shard_map(local, mesh=mesh, in_specs=in_specs, out_specs=out_specs, check_vma=False)
```

profile of v0, /device:TPU:1, one launch (start us, length us, event | category | flops | bytes accessed | tf_op | source)
XLA Modules:
  0.0 3658.7 jit_solution(18283201133194644268)
XLA Ops:
  25.4 90.4 %all-gather.10.cloned.1.call-done = bf16[2048,2048]{1,0:T(8,128)(2,1)} async-done(((bf16[1024,2048]{1,0:T(8,128)(2,1)}), bf16[2048,2048]{1,0:T(8,128)(2,1)}) %all-gather.10.cloned.1.call-update) | async-done | bytes 8388624 | tf_op jit(solution)/shard_map/all_gather | solution.py:114
  123.8 97.6 %all-gather.14.cloned.1.call-done = bf16[2048,2048]{1,0:T(8,128)(2,1)} async-done(((bf16[1024,2048]{1,0:T(8,128)(2,1)}), bf16[2048,2048]{1,0:T(8,128)(2,1)}) %all-gather.14.cloned.1.call-update) | async-done | bytes 8388624 | tf_op jit(solution)/shard_map/all_gather | solution.py:113
  237.7 89.4 %all-gather.16.cloned.1.call-done = bf16[2048,2048]{1,0:T(8,128)(2,1)} async-done(((bf16[1024,2048]{1,0:T(8,128)(2,1)}), bf16[2048,2048]{1,0:T(8,128)(2,1)}) %all-gather.16.cloned.1.call-update) | async-done | bytes 8388624 | tf_op jit(solution)/shard_map/all_gather | solution.py:115
  336.4 96.1 %all-gather.20.cloned.1.call-done = bf16[2048,2048]{1,0:T(8,128)(2,1)} async-done(((bf16[1024,2048]{1,0:T(8,128)(2,1)}), bf16[2048,2048]{1,0:T(8,128)(2,1)}) %all-gather.20.cloned.1.call-update) | async-done | bytes 8388624 | tf_op jit(solution)/shard_map/all_gather | solution.py:179
  443.9 71.3 %all-gather.12.cloned.1.call-done = bf16[1024,2048]{0,1:T(8,128)(2,1)} async-done(((bf16[256,2048]{0,1:T(8,128)(2,1)}), bf16[1024,2048]{0,1:T(8,128)(2,1)}) %all-gather.12.cloned.1.call-update) | async-done | bytes 4194320 | tf_op jit(solution)/shard_map/all_gather | solution.py:143
  522.0 74.0 %all-gather.18.cloned.1.call-done = bf16[1024,2048]{1,0:T(8,128)(2,1)} async-done(((bf16[256,2048]{1,0:T(8,128)(2,1)}), bf16[1024,2048]{1,0:T(8,128)(2,1)}) %all-gather.18.cloned.1.call-update) | async-done | bytes 4194320 | tf_op jit(solution)/shard_map/all_gather | solution.py:144
  596.1 13.5 conditional.1
  682.3 17.1 reduce-scatter.6.cloned.1.call-done
  717.4 62.3 %reduce-scatter.8.cloned.1.call-done = bf16[256,2048]{0,1:T(8,128)(2,1)} async-done(((bf16[1024,2048]{0,1:T(8,128)(2,1)}), bf16[256,2048]{0,1:T(8,128)(2,1)}) %reduce-scatter.8.cloned.1.call-update) | async-done | bytes 1048592 | tf_op jit(solution)/shard_map/reduce_scatter | solution.py:227
  779.7 16.6 convolution_convert_fusion.1
  796.3 374.0 %all-gather.22.cloned.1.call-done = bf16[2048,8192]{1,0:T(8,128)(2,1)} async-done(((bf16[1024,8192]{1,0:T(8,128)(2,1)}), bf16[2048,8192]{1,0:T(8,128)(2,1)}) %all-gather.22.cloned.1.call-update) | async-done | bytes 33554448 | tf_op jit(solution)/shard_map/all_gather | solution.py:116
  1170.3 32.9 multiply_convert_fusion.2
  1203.2 19.1 convert_bitcast_fusion
  1222.3 338.0 %all-gather.24.cloned.1.call-done = bf16[2048,8192]{1,0:T(8,128)(2,1)} async-done(((bf16[1024,8192]{1,0:T(8,128)(2,1)}), bf16[2048,8192]{1,0:T(8,128)(2,1)}) %all-gather.24.cloned.1.call-update) | async-done | bytes 33554448 | tf_op jit(solution)/shard_map/all_gather | solution.py:179
  1560.3 32.5 fusion.95
  1592.8 16.8 convolution_convert_fusion
  1609.5 65.9 %pad_maximum_fusion = bf16[2048,24576]{1,0:T(8,128)(2,1)} fusion(bf16[2048,8192]{1,0:T(8,128)(2,1)} %convert_bitcast_fusion, bf16[2048,8192]{1,0:T(8,128)(2,1)} %convolution_convert_fusion, bf16[2048,2048]{1,0:T(8,128)(2,1)} %copy.105, bf16[2048,6144]{1,0:T(8,128)(2,1)} %convolution_convert_fusion.1), kind=kLoop, calls=%fused_computation.16 | loop fusion | flops 402653184 | bytes 201326592 | tf_op jit(solution)/shard_map/concatenate | solution.py:305
  1675.5 1088.3 %reduce-scatter.10.cloned.1.call-done = bf16[1024,24576]{1,0:T(8,128)(2,1)} async-done(((bf16[2048,24576]{1,0:T(8,128)(2,1)}), bf16[1024,24576]{1,0:T(8,128)(2,1)}) %reduce-scatter.10.cloned.1.call-update) | async-done | bytes 50331664
  2797.7 17.5 fusion.99
  2832.1 63.0 %all-reduce.11 = (bf16[1024]{0:T(1024)(128)(2,1)S(1)}, bf16[1024]{0:T(1024)(128)(2,1)S(1)}, bf16[1024]{0:T(1024)(128)(2,1)S(1)}, bf16[1024]{0:T(1024)(128)(2,1)S...) all-reduce(bf16[1024]{0:T(1024)(128)(2,1)S(1)} %dynamic-slice.1, ...), channel_id=1, replica_groups=mesh['dp'=4,'ctx'=4,'fsdp'=2] {'dp','ctx'}, use_global_device_ids=true, to_apply=%region_15.16 | all-reduce | flops 11520 | bytes 46080 | tf_op jit(solution)/shard_map/psum | solution.py:328
  2904.8 18.4 fusion.54
  2923.1 679.4 %all-reduce.15.cloned.1.call-done = bf16[1024,24576]{1,0:T(8,128)(2,1)} async-done(((bf16[1024,24576]{1,0:T(8,128)(2,1)}), bf16[1024,24576]{1,0:T(8,128)(2,1)}) %all-reduce.15.cloned.1.call-update) | async-done | bytes 50331664 | tf_op jit(solution)/shard_map/psum | solution.py:327
  3602.5 15.3 fusion.91
  3617.8 33.3 fusion.90
  (204 shorter events, 232.6 us)
Async XLA Ops:
  7.2 108.5 %all-gather.10.cloned.1.call-start = ((), (), s32[]{:S(2)}) async-start(), calls=%async_computation.3 | async-start | bytes 12582912 | tf_op jit(solution)/shard_map/all_gather | solution.py:114
  8.0 213.4 %all-gather.14.cloned.1.call-start = ((), (), s32[]{:S(2)}) async-start(), calls=%async_computation.5 | async-start | bytes 12582912 | tf_op jit(solution)/shard_map/all_gather | solution.py:113
  8.7 318.3 %all-gather.16.cloned.1.call-start = ((), (), s32[]{:S(2)}) async-start(), calls=%async_computation.6 | async-start | bytes 12582912 | tf_op jit(solution)/shard_map/all_gather | solution.py:115
  9.5 423.0 %all-gather.20.cloned.1.call-start = ((), (), s32[]{:S(2)}) async-start(), calls=%async_computation.8 | async-start | bytes 12582912 | tf_op jit(solution)/shard_map/all_gather | solution.py:179
  10.0 505.2 %all-gather.12.cloned.1.call-start = ((), (), s32[]{:S(2)}) async-start(), calls=%async_computation.4 | async-start | bytes 5242880 | tf_op jit(solution)/shard_map/all_gather | solution.py:143
  20.2 759.4 %copy-start.13 = (f32[2048]{0:T(1024)}, f32[2048]{0:T(1024)S(1)}, u32[]{:S(2)}) copy-start(f32[2048]{0:T(1024)S(1)} %all_gather.62) | copy-start | bytes 24580
  23.7 303.3 %copy-start.17 = (f32[256]{0:T(256)}, f32[256]{0:T(256)S(1)}, u32[]{:S(2)}) copy-start(f32[256]{0:T(256)S(1)} %broadcast_multiply_fusion) | copy-start | bytes 3076
  24.1 97.4 %copy-start.25 = (f32[256]{0:T(256)}, f32[256]{0:T(256)S(1)}, u32[]{:S(2)}) copy-start(f32[256]{0:T(256)S(1)} %fusion.61) | copy-start | bytes 3076
  24.1 302.9 %copy-start.19 = (f32[256]{0:T(256)}, f32[256]{0:T(256)S(1)}, u32[]{:S(2)}) copy-start(f32[256]{0:T(256)S(1)} %fusion.74) | copy-start | bytes 3076
  233.9 362.2 %all-gather.18.cloned.1.call-start = ((), (), s32[]{:S(2)}) async-start(), calls=%async_computation.7 | async-start | bytes 5242880 | tf_op jit(solution)/shard_map/all_gather | solution.py:144
  237.7 194.8 %copy-start.1 = (bf16[1,256,2048]{2,1,0:T(8,128)(2,1)S(1)}, bf16[1,256,2048]{2,1,0:T(8,128)(2,1)}, u32[]{:S(2)}) copy-start(bf16[1,256,2048]{2,1,0:T(8,128)(2,1)} %param.21) | copy-start | bytes 3145732
  333.8 365.6 %reduce-scatter.6.cloned.1.call-start = ((), (), s32[]{:S(2)}) async-start(), calls=%async_computation.11 | async-start | bytes 5242880 | tf_op jit(solution)/shard_map/reduce_scatter | solution.py:221
  623.9 155.8 %reduce-scatter.8.cloned.1.call-start = ((), (), s32[]{:S(2)}) async-start(), calls=%async_computation.12 | async-start | bytes 5242880 | tf_op jit(solution)/shard_map/reduce_scatter | solution.py:227
  644.5 525.8 %all-gather.22.cloned.1.call-start = ((), (), s32[]{:S(2)}) async-start(), calls=%async_computation.9 | async-start | bytes 50331648 | tf_op jit(solution)/shard_map/all_gather | solution.py:116
  645.3 915.0 %all-gather.24.cloned.1.call-start = ((), (), s32[]{:S(2)}) async-start(), calls=%async_computation.10 | async-start | bytes 50331648 | tf_op jit(solution)/shard_map/all_gather | solution.py:179
  645.9 2118.0 %reduce-scatter.10.cloned.1.call-start = ((), (), s32[]{:S(2)}) async-start(), calls=%async_computation.14 | async-start | bytes 150994944
  705.8 73.9 %copy-start.18 = (f32[256]{0:T(256)S(1)}, f32[256]{0:T(256)}, u32[]{:S(2)}) copy-start(f32[256]{0:T(256)} %copy-done.17) | copy-start | bytes 3076
  705.8 73.9 %copy-start.20 = (f32[256]{0:T(256)S(1)}, f32[256]{0:T(256)}, u32[]{:S(2)}) copy-start(f32[256]{0:T(256)} %copy-done.19) | copy-start | bytes 3076
  717.4 78.9 %copy-start.7 = (bf16[256,8,256]{0,2,1:T(8,128)(2,1)}, bf16[256,8,256]{0,2,1:T(8,128)(2,1)S(1)}, u32[]{:S(2)}) copy-start(bf16[256,8,256]{0,2,1:T(8,128)(2,1)S(1)} %maximum_convert_fusion.1) | copy-start | bytes 3145732
  779.7 390.6 %copy-start.15 = (f32[2048]{0:T(1024)S(1)}, f32[2048]{0:T(1024)}, u32[]{:S(2)}) copy-start(f32[2048]{0:T(1024)} %all_gather.73) | copy-start | bytes 24580
  779.7 390.6 %copy-start.16 = (f32[2048]{0:T(1024)S(1)}, f32[2048]{0:T(1024)}, u32[]{:S(2)}) copy-start(f32[2048]{0:T(1024)} %all_gather.74) | copy-start | bytes 24580
  779.7 390.6 %copy-start.21 = (f32[8192]{0:T(1024)S(1)}, f32[8192]{0:T(1024)}, u32[]{:S(2)}) copy-start(f32[8192]{0:T(1024)} %all_gather.76) | copy-start | bytes 98308
  1675.5 1927.0 %all-reduce.15.cloned.1.call-start = ((), (), s32[]{:S(2)}) async-start(), calls=%async_computation.13 | async-start | bytes 100663296 | tf_op jit(solution)/shard_map/psum | solution.py:327
  2899.2 751.8 %copy-start.24 = (f32[1024]{0:T(1024)}, f32[1024]{0:T(1024)S(1)}, u32[]{:S(2)}) copy-start(f32[1024]{0:T(1024)S(1)} %convert_element_type.226) | copy-start | bytes 12292
  (26 other events, 205.6 us)
Sparse Core Ops, SparseCore 0:
  9.6 106.1 all-gather.9
  117.3 103.9 all-gather.13
  222.9 104.0 all-gather.15
  328.4 103.9 all-gather.19
  434.5 80.6 all-gather.11
  517.2 78.8 all-gather.17
  624.0 75.2 reduce-scatter.5
  702.4 77.2 reduce-scatter.7
  781.2 388.9 all-gather.21
  1171.7 388.5 all-gather.23
  1675.6 1088.2 reduce-scatter.9
  2768.0 834.4 all-reduce.14
where the time goes:
time: 3670 us; the launch traced here: 3660 us
  waiting for transfers between devices  3080 us (84%)
  matrix products  253 us (7%)
  blocking collectives  104 us (3%)
  other arithmetic  103 us (3%)
  local copies, waits for them, and re-layouts  87.2 us (2%)
    unnamed x13, waiting for transfers between devices  1090 us
    psum x1, waiting for transfers between devices, local(): lax.psum(fsdp_shard, ('dp', 'ctx')).astype(jnp.float32)  679 us
    all_gather x2, waiting for transfers between devices, local(): lax.all_gather((w_out, w_down), 'fsdp', axis=0, tiled=True)  434 us
    all_gather x1, waiting for transfers between devices, local(): piece_u = lax.all_gather(w_up, 'fsdp', axis=0, tiled=True)  374 us
    all_gather x1, waiting for transfers between devices, local(): piece_q = lax.all_gather(w_query, 'fsdp', axis=0, tiled=True)  97.6 us
    all_gather x1, waiting for transfers between devices, local(): piece_k = lax.all_gather(w_key, 'fsdp', axis=0, tiled=True)  90.4 us
    all_gather x1, waiting for transfers between devices, local(): piece_v = lax.all_gather(w_value, 'fsdp', axis=0, tiled=True)  89.4 us
    all_gather x1, waiting for transfers between devices, local(): piece_v = lax.all_gather(value_low, 'ctx', axis=0, tiled=True)  74 us
  transfers between devices with their start and end apart: 12, of which 12 were waited for; matrix products, arithmetic and copies ran while one was open for 7% of the time, Pallas kernels for 0%

commit v1 on v0

v1 whole, which is shorter than its diff:
```python
import functools
import math

import jax
import jax.numpy as jnp
from jax import lax
from jax.experimental import pallas as pl
from jax.experimental.pallas import tpu as pltpu
from jax.sharding import PartitionSpec as P

HEAD_DIM = 256
ROT = 64
HALF = ROT // 2
LANES = 128
CORES = 2
norm_eps = 1e-05
masked_score = -1e30
MIB = 1 << 20
f32 = jnp.float32
bf16 = jnp.bfloat16
SCALE = 1.0 / math.sqrt(HEAD_DIM)
F_AT, J_AT, Y_AT, Z_AT, C_AT = range(5)


def dot(left, right, dims):
    return lax.dot_general(left, right, (dims, ((), ())), preferred_element_type=f32)


def mm(left, right):
    return dot(left, right, ((1,), (0,)))


def mm_rows(left, right):
    return dot(left, right, ((1,), (1,)))


def mm_tokens(left, right):
    return dot(left, right, ((0,), (0,)))


def array(shape, dtype):
    return jax.ShapeDtypeStruct(shape, dtype)


ANY = pl.BlockSpec(memory_space=pl.ANY)
PLANNED = {
    "join": 2,
    "forward": 18,
    "attend": 2,
    "branch": 10,
    "sum_mixed": 4,
    "down_back": 10,
    "grad_down": 9,
    "grad_up": 9,
    "grad_att": 9,
    "attend_back": 6,
    "back": 13,
    "sum_back": 4,
    "sum_fsdp": 2,
    "sum_pairs": 8,
    "sum_small": 1,
    "pin": 15,
    "place": 4,
    "mixed": 3,
    "grad_tokens": 4,
}


class Chain:
    def __init__(self, at):
        self.at = at
        self.last = None

    def __call__(self, kernel, outs, grid, in_specs, out_specs, operands, aliases=None, scratch=(), name=None, limit=50, after=()):
        n_in, n_out = len(operands), len(outs)
        extra = ([] if self.last is None else [self.last]) + list(after)

        def body(at_ref, *refs):
            ins = refs[:n_in]
            made = refs[n_in + len(extra) :]
            kernel(at_ref, ins, made[:n_out], made[n_out + 1 :])

        result = pl.pallas_call(
            body,
            out_shape=tuple(outs) + (array((8, LANES), f32),),
            grid_spec=pltpu.PrefetchScalarGridSpec(
                num_scalar_prefetch=1,
                grid=grid,
                in_specs=list(in_specs) + [ANY] * len(extra),
                out_specs=list(out_specs) + [ANY],
                scratch_shapes=list(scratch),
            ),
            input_output_aliases=aliases or {},
            compiler_params=pltpu.CompilerParams(vmem_limit_bytes=limit * MIB),
            cost_estimate=pl.CostEstimate(
                flops=int(1.15e4 * PLANNED[name]), bytes_accessed=1, transcendentals=0
            ),
            name=name,
        )(self.at, *operands, *extra)
        self.last = result[-1]
        return result[:-1]


def rem(a, n):
    return lax.rem(a, jnp.int32(n))


def columns(at_ref, k, n_f, rows):
    block = rem(at_ref[F_AT] + n_f - k, n_f)
    return pl.ds(pl.multiple_of(block * rows, rows), rows)


def turn(v, cos_t, sin_a, sin_b):
    low = v[:, :LANES]
    low = low * cos_t + pltpu.roll(low, LANES - HALF, 1) * sin_a + pltpu.roll(low, HALF, 1) * sin_b
    return jnp.concatenate([low, v[:, LANES:]], axis=1)


def shift_perm(count, step):
    return [(i, (i + step) % count) for i in range(count)]


def local(
    n_dp,
    n_ctx,
    n_f,
    tokens,
    cotangent,
    norm1_gain,
    norm1_bias,
    norm2_gain,
    norm2_bias,
    w_query,
    w_key,
    w_value,
    b_query,
    b_key,
    b_value,
    w_out,
    b_out,
    w_up,
    b_up,
    w_down,
    b_down,
):
    n_y = n_dp // CORES
    dp_idx, z_idx, f_idx = lax.axis_index("dp"), lax.axis_index("ctx"), lax.axis_index("fsdp")
    y_idx, c_idx = dp_idx // CORES, dp_idx % CORES
    splits = n_ctx * CORES
    j_idx = z_idx * CORES + c_idx
    block_rows, width = tokens.shape[1], tokens.shape[2]
    length = block_rows * n_ctx
    hidden = w_up.shape[1]
    heads = width // HEAD_DIM
    rows = width // n_f
    n_att, n_hid = width // splits, hidden // splits
    assert n_att == HEAD_DIM and n_ctx == 4
    n_qkv = 3 * n_att
    half_hid = n_hid // 2
    at = jnp.stack([f_idx, j_idx, y_idx, z_idx, c_idx]).astype(jnp.int32)
    run = Chain(at)

    def core_swap(value):
        return lax.ppermute(value, "dp", [(i, i ^ 1) for i in range(n_dp)])

    def over_y(value, step):
        return lax.ppermute(value, "dp", shift_perm(n_dp, CORES * step))

    def over_z(value, step):
        return lax.ppermute(value, "ctx", shift_perm(n_ctx, step))

    def over_f(value, step):
        return lax.ppermute(value, "fsdp", shift_perm(n_f, step))

    def mine(w, n):
        return lax.dynamic_slice_in_dim(w, j_idx * n, n, axis=1)

    small = [norm1_gain, norm1_bias, norm2_gain, norm2_bias, b_query, b_key, b_value, b_out + b_down, b_up]
    sizes = [s.shape[0] for s in small]
    ends = [sum(sizes[:i]) for i in range(len(sizes) + 1)]
    small_own = jnp.concatenate(small)
    small_got = [small_own] + [over_f(small_own, k) for k in range(1, n_f)]

    own_tok = lax.all_gather(tokens[0], "ctx", axis=0, tiled=True)
    own_cot = lax.all_gather(cotangent[0], "ctx", axis=0, tiled=True)
    cot = (own_cot, core_swap(own_cot))

    def pin(value, after=()):
        return run(lambda *a: None, [array(value.shape, value.dtype)], (1,), [ANY], [ANY], [value], aliases={1: 0}, name="pin", limit=4, after=after)[0]

    def fetch(part):
        return [over_f(part, k) for k in range(1, n_f)]

    y_part = rows // n_y
    got_u = fetch(lax.dynamic_slice(w_up, (y_idx * y_part, j_idx * n_hid), (y_part, n_hid)))
    got_qkv = fetch(jnp.concatenate([mine(w_query, n_att), mine(w_key, n_att), mine(w_value, n_att)], axis=1))
    got_do = fetch(jnp.concatenate([mine(w_down, n_hid), mine(w_out, n_att)], axis=1))

    def whole(i):
        pieces = [g[ends[i] : ends[i + 1]] for g in small_got]
        if n_f == 2:
            return jnp.concatenate([jnp.where(f_idx == m, pieces[0], pieces[1]) for m in range(2)])
        rolled = jnp.stack(pieces[::-1])
        return jnp.roll(rolled, f_idx + 1, axis=0).reshape(-1)

    gain1, shift1, gain2, shift2, bq, bk, bv, b_last, bu = [whole(i) for i in range(len(small))]

    def part(vec, n):
        return lax.dynamic_slice_in_dim(vec, j_idx * n, n, axis=0)

    def eight(vec):
        return jnp.broadcast_to(vec[None], (8, vec.shape[0]))

    vecs = jnp.concatenate([jnp.stack([gain1, shift1, gain2, shift2]), jnp.zeros((4, width), f32)])
    key_shift = jnp.pad(part(bk, ROT), (0, HEAD_DIM - ROT))
    bias_qkv = eight(jnp.concatenate([part(bq, n_att), key_shift, part(bv, n_att)]))
    bias_up = eight(part(bu, n_hid))
    bias_last = eight(b_last)
    positions = jnp.arange(length, dtype=f32)
    inverse = 10000.0 ** (-2.0 * jnp.arange(HALF, dtype=f32) / ROT)
    angles = positions[:, None] * inverse[None, :]
    cosine, sine = jnp.cos(angles), jnp.sin(angles)
    none = jnp.zeros((length, LANES - ROT), f32)
    zero = jnp.zeros_like(sine)
    tables = (
        jnp.concatenate([cosine, cosine, none + 1.0], axis=1),
        jnp.concatenate([-sine, zero, none], axis=1),
        jnp.concatenate([zero, sine, none], axis=1),
    )

    def join_kernel(at_ref, ins, outs, scratch):
        for k, r in enumerate(ins):

            @pl.when(pl.program_id(0) == k)
            def _(r=r):
                outs[0][0] = r[...]

    def share(piece):
        piece = pin(piece)
        parts = [piece] + [over_y(piece, k) for k in range(1, n_y)]
        joined = run(
            join_kernel,
            [array((n_y, y_part, n_hid), bf16)],
            (n_y,),
            [pl.BlockSpec((y_part, n_hid), lambda i, at: (0, 0))] * n_y,
            [pl.BlockSpec((1, y_part, n_hid), lambda i, at: (rem(at[Y_AT] + n_y - i, n_y), 0, 0))],
            parts,
            name="join",
            limit=16,
        )[0]
        return joined.reshape(rows, n_hid)

    vecs, bias_qkv, bias_up = pin(vecs), pin(bias_qkv), pin(bias_up)
    tables = tuple(pin(t) for t in tables)
    got_u = [share(g) for g in got_u]
    own_tok = pin(own_tok)
    tok = ([own_tok], [core_swap(own_tok[m * block_rows : (m + 1) * block_rows]) for m in range(n_ctx)])

    def rows_of(n, w):
        return pl.BlockSpec((n, w), lambda i, at: (i, 0))

    def fixed(n, w):
        return pl.BlockSpec((n, w), lambda i, at: (0, 0))

    def column(n, w):
        return pl.BlockSpec((n, w), lambda i, at: (0, at[J_AT]))

    own_qkv = [w_query, w_key, w_value]
    qkv_specs = [column(rows, n_att)] * 3 + [fixed(rows, n_qkv)] * (n_f - 1)
    u_specs = [column(rows, n_hid)] + [fixed(rows, n_hid)] * (n_f - 1)
    do_specs = [column(rows, n_hid), column(rows, n_att)] + [fixed(rows, n_hid + n_att)] * (n_f - 1)
    step = min(256, length)
    tok_grid = (length // step,)
    n_vec = len(tables)

    def forward_kernel(n_x, at_ref, ins, outs, scratch):
        x_refs, ins = ins[:n_x], ins[n_x:]
        vec_ref, cos_ref, sa_ref, sb_ref, bqkv_ref, bu_ref = ins[:6]
        wu = ins[6 : 6 + n_f]
        wq, wk, wv = ins[6 + n_f : 9 + n_f]
        w_other = ins[9 + n_f :]
        a1_ref, a2_ref, act_ref, slope_ref, qkv_ref = outs

        def normalize(x_ref):
            x = x_ref[...].astype(f32)
            center = x - jnp.mean(x, axis=-1, keepdims=True)
            spread = jnp.mean(center * center, axis=-1, keepdims=True)
            n = center * lax.rsqrt(spread + norm_eps)
            a1_ref[...] = (n * vec_ref[0:1] + vec_ref[1:2]).astype(bf16)
            a2_ref[...] = (n * vec_ref[2:3] + vec_ref[3:4]).astype(bf16)

        each = length // step // n_x
        for m, x_ref in enumerate(x_refs):
            if n_x == 1:
                normalize(x_ref)
            else:
                pl.when(pl.program_id(0) // each == m)(functools.partial(normalize, x_ref))
        h = jnp.broadcast_to(bu_ref[0:1], (step, n_hid))
        for k in range(n_f):
            h = h + mm(a2_ref[:, columns(at_ref, k, n_f, rows)], wu[k][...])
        cdf = 0.5 * (1.0 + lax.erf(h * (1.0 / math.sqrt(2.0))))
        pdf = jnp.exp(-0.5 * h * h) * (1.0 / math.sqrt(2.0 * math.pi))
        act_ref[...] = (h * cdf).astype(bf16)
        slope_ref[...] = (cdf + h * pdf).astype(bf16)
        cos_t, sa, sb = cos_ref[...], sa_ref[...], sb_ref[...]
        for m, w_own in enumerate((wq, wk, wv)):
            lanes = slice(m * n_att, (m + 1) * n_att)
            v = mm(a1_ref[:, columns(at_ref, 0, n_f, rows)], w_own[...]) + bqkv_ref[0:1, lanes]
            for k in range(1, n_f):
                v = v + mm(a1_ref[:, columns(at_ref, k, n_f, rows)], w_other[k - 1][:, lanes])
            qkv_ref[:, lanes] = (turn(v, cos_t, sa, sb) if m < 2 else v).astype(bf16)

    def forward(xs):
        each = length // step // len(xs)

        def rows_in(m):
            return pl.BlockSpec((step, width), lambda i, at: (jnp.clip(i - m * each, 0, each - 1), 0))

        return run(
            functools.partial(forward_kernel, len(xs)),
            [array((length, width), bf16)] * 2 + [array((length, n_hid), bf16)] * 2 + [array((length, n_qkv), bf16)],
            tok_grid,
            [rows_in(m) for m in range(len(xs))]
            + [fixed(8, width)]
            + [rows_of(step, LANES)] * n_vec
            + [fixed(8, n_qkv), fixed(8, n_hid)]
            + u_specs
            + qkv_specs,
            [rows_of(step, width)] * 2 + [rows_of(step, n_hid)] * 2 + [rows_of(step, n_qkv)],
            [*xs, vecs, *tables, bias_qkv, bias_up, w_up, *got_u, *own_qkv, *got_qkv],
            name="forward",
        )

    q_block = min(256, length)

    def masked(lo, hi):
        rows_at = lo + lax.broadcasted_iota(jnp.int32, (hi - lo, hi), 0)
        return lax.broadcasted_iota(jnp.int32, (hi - lo, hi), 1) <= rows_at

    def attend_kernel(at_ref, ins, outs, scratch):
        (qkv_ref,) = ins
        att_ref, lse_ref = outs
        for lo in range(0, length, q_block):
            hi = lo + q_block
            s = mm_rows(qkv_ref[lo:hi, :n_att], qkv_ref[:hi, n_att : 2 * n_att]) * SCALE
            allowed = masked(lo, hi)
            s = jnp.where(allowed, s, masked_score)
            top = jnp.max(s, axis=-1, keepdims=True)
            e = jnp.where(allowed, jnp.exp(s - top), 0.0)
            total = jnp.sum(e, axis=-1, keepdims=True)
            att_ref[lo:hi] = (mm(e.astype(bf16), qkv_ref[:hi, 2 * n_att :]) / total).astype(bf16)
            lse_ref[lo:hi] = jnp.broadcast_to(top + jnp.log(total), (q_block, LANES))

    def attend(qkv):
        return run(
            attend_kernel,
            [array((length, n_att), bf16), array((length, LANES), f32)],
            (1,),
            [fixed(length, n_qkv)],
            [fixed(length, n_att), fixed(length, LANES)],
            [qkv],
            name="attend",
        )

    def attend_back_kernel(at_ref, ins, outs, scratch):
        qkv_ref, do_ref, lse_ref, cos_ref, sa_ref, sb_ref = ins
        grad_ref, sum_ref = outs
        dk_acc, dv_acc = scratch
        q_sum = jnp.zeros((1, n_att), f32)
        for lo in range(0, length, q_block):
            hi = lo + q_block
            qi, ki, vi = qkv_ref[lo:hi, :n_att], qkv_ref[:hi, n_att : 2 * n_att], qkv_ref[:hi, 2 * n_att :]
            do = do_ref[lo:hi]
            s = mm_rows(qi, ki) * SCALE
            chance = jnp.where(masked(lo, hi), jnp.exp(s - lse_ref[lo:hi, 0:1]), 0.0)
            d_chance = mm_rows(do, vi)
            row_dot = jnp.sum(chance * d_chance, axis=-1, keepdims=True)
            ds = (chance * (d_chance - row_dot)).astype(bf16)
            dq = turn(mm(ds, ki) * SCALE, cos_ref[lo:hi], -sa_ref[lo:hi], -sb_ref[lo:hi]).astype(bf16)
            grad_ref[lo:hi, :n_att] = dq
            q_sum = q_sum + jnp.sum(dq.astype(f32), axis=0, keepdims=True)
            dk, dv = mm_tokens(ds, qi), mm_tokens(chance.astype(bf16), do)
            if lo > 0:
                dk_acc[:lo] += dk[:lo]
                dv_acc[:lo] += dv[:lo]
            dk_acc[lo:hi] = dk[lo:]
            dv_acc[lo:hi] = dv[lo:]
        dk = turn(dk_acc[...] * SCALE, cos_ref[...], -sa_ref[...], -sb_ref[...]).astype(bf16)
        dv = dv_acc[...].astype(bf16)
        grad_ref[:, n_att : 2 * n_att] = dk
        grad_ref[:, 2 * n_att :] = dv
        sums = (q_sum, jnp.sum(dk.astype(f32), axis=0, keepdims=True), jnp.sum(dv.astype(f32), axis=0, keepdims=True))
        for m, total in enumerate(sums):
            sum_ref[:, m * n_att : (m + 1) * n_att] = jnp.broadcast_to(total, (8, n_att))

    def attend_back(qkv, do, lse):
        return run(
            attend_back_kernel,
            [array((length, n_qkv), bf16), array((8, n_qkv), f32)],
            (1,),
            [fixed(length, n_qkv), fixed(length, n_att)] + [fixed(length, LANES)] * (1 + n_vec),
            [fixed(length, n_qkv), fixed(8, n_qkv)],
            [qkv, do, lse, *tables],
            scratch=[pltpu.VMEM((length, n_att), f32)] * 2,
            name="attend_back",
        )

    def down_out(refs, k):
        if k == 0:
            return refs[0][...], refs[1][...]
        return refs[1 + k][:, :n_hid], refs[1 + k][:, n_hid:]

    def branch_kernel(at_ref, ins, outs, scratch):
        act_ref, att_ref = ins[:2]
        for k in range(n_f):
            wd, wo = down_out(ins[2:], k)
            value = mm_rows(act_ref[...], wd) + mm_rows(att_ref[...], wo)
            outs[0][:, columns(at_ref, k, n_f, rows)] = value.astype(bf16)

    def branch(act, att):
        return run(
            branch_kernel,
            [array((length, width), bf16)],
            tok_grid,
            [rows_of(step, n_hid), rows_of(step, n_att)] + do_specs,
            [rows_of(step, width)],
            [act, att, w_down, w_out, *got_do],
            name="branch",
        )[0]

    def split_kernel(count, at_ref, ins, outs, scratch):
        for k in range(count):

            @pl.when(pl.program_id(0) == k)
            def _(k=k):
                total = ins[0][...].astype(f32)
                for r in ins[1:]:
                    total = total + r[...].astype(f32)
                outs[k][...] = total.astype(outs[k].dtype)

    def split_sum(values, count, where, name):
        n, w = values[0].shape
        spec = pl.BlockSpec((n // count, w), lambda i, at: (i if where is None else rem(at[where] + i, count), 0))
        return run(
            functools.partial(split_kernel, count),
            [array((n // count, w), f32 if k == 0 else bf16) for k in range(count)],
            (count,),
            [spec] * len(values),
            [fixed(n // count, w)] * count,
            values,
            name=name,
            limit=16,
        )

    def add_kernel(at_ref, ins, outs, scratch):
        total = ins[0][...].astype(f32)
        for r in ins[1:]:
            total = total + r[...].astype(f32)
        outs[0][...] = total.astype(outs[0].dtype)

    def add(values, dtype, name):
        n, w = values[0].shape
        m = n // 2 if n % 32 == 0 else n
        return run(
            add_kernel,
            [array((n, w), dtype)],
            (n // m,),
            [rows_of(m, w)] * len(values),
            [rows_of(m, w)],
            values,
            name=name,
            limit=16,
        )[0]

    def to_owners(own, other_got, name):
        return lax.psum_scatter(add([own, other_got], bf16, name), "ctx", scatter_dimension=0, tiled=True)

    def down_back_kernel(at_ref, ins, outs, scratch):
        c_ref, slope_ref = ins[:2]
        pre_ref, do_ref, sum_ref = outs
        g_act = jnp.zeros((step, n_hid), f32)
        g_att = jnp.zeros((step, n_att), f32)
        for k in range(n_f):
            c = c_ref[:, columns(at_ref, k, n_f, rows)]
            wd, wo = down_out(ins[2:], k)
            g_act = g_act + mm(c, wd)
            g_att = g_att + mm(c, wo)
        pre = (g_act * slope_ref[...].astype(f32)).astype(bf16)
        pre_ref[...] = pre
        do_ref[...] = g_att.astype(bf16)
        total = jnp.broadcast_to(jnp.sum(pre.astype(f32), axis=0, keepdims=True), (8, n_hid))

        @pl.when(pl.program_id(0) == 0)
        def _():
            sum_ref[...] = total

        @pl.when(pl.program_id(0) > 0)
        def _():
            sum_ref[...] += total

    def down_back(c, slope):
        return run(
            down_back_kernel,
            [array((length, n_hid), bf16), array((length, n_att), bf16), array((8, n_hid), f32)],
            tok_grid,
            [rows_of(step, width), rows_of(step, n_hid)] + do_specs,
            [rows_of(step, n_hid), rows_of(step, n_att), fixed(8, n_hid)],
            [c, slope, w_down, w_out, *got_do],
            name="down_back",
        )

    def back_kernel(at_ref, ins, outs, scratch):
        dqkv_ref, dpre_ref, vec_ref = ins[:3]
        wq, wk, wv = ins[3:6]
        w_other, wu = ins[6 : 5 + n_f], ins[5 + n_f :]
        for k in range(n_f):
            cols = columns(at_ref, k, n_f, rows)
            if k == 0:
                first = mm_rows(dqkv_ref[:, :n_att], wq[...])
                first = first + mm_rows(dqkv_ref[:, n_att : 2 * n_att], wk[...])
                first = first + mm_rows(dqkv_ref[:, 2 * n_att :], wv[...])
            else:
                first = mm_rows(dqkv_ref[...], w_other[k - 1][...])
            second = mm_rows(dpre_ref[...], wu[k][...])
            outs[0][:, cols] = (first * vec_ref[0:1, cols] + second * vec_ref[2:3, cols]).astype(bf16)

    def back(dqkv, dpre):
        return run(
            back_kernel,
            [array((length, width), bf16)],
            tok_grid,
            [rows_of(step, n_qkv), rows_of(step, n_hid), fixed(8, width)] + qkv_specs + u_specs,
            [rows_of(step, width)],
            [dqkv, dpre, vecs, *own_qkv, *got_qkv, w_up, *got_u],
            name="back",
        )[0]

    g_step = min(256, rows)
    per = rows // g_step

    def grads_kernel(n_pairs, n_w, chunks, at_ref, ins, outs, scratch):
        pieces = []
        for i in range(n_pairs):
            a0, a1, g0, g1 = ins[4 * i : 4 * i + 4]
            pieces.append(mm_tokens(a0[...], g0[...]) + mm_tokens(a1[...], g1[...]))
        start = 0
        full = pieces[0] if n_pairs == 1 else jnp.concatenate(pieces, axis=1)
        for out, n in zip(outs, chunks):
            out[...] = full[:, start : start + n].astype(out.dtype)
            start += n
        if n_w:
            weights = ins[4 * n_pairs : 4 * n_pairs + n_w]
            sums = ins[4 * n_pairs + n_w :]
            g_sum = sums[0][0:1] + sums[1][0:1]
            gain = jnp.zeros((g_step, 1), f32)
            shift = jnp.zeros((g_step, 1), f32)
            start = 0
            for w_ref in weights:
                w = w_ref[...].astype(f32)
                n = w.shape[1]
                gain = gain + jnp.sum(w * full[:, start : start + n], axis=1, keepdims=True)
                shift = shift + jnp.sum(w * g_sum[:, start : start + n], axis=1, keepdims=True)
                start += n
            lane = lax.broadcasted_iota(jnp.int32, (g_step, LANES), 1)
            outs[-1][...] = jnp.where(lane == 0, gain, jnp.where(lane == 1, shift, 0.0))

    def grads(pairs, chunks, k, weights, sums, name):
        def left(i, at):
            return (0, rem(at[F_AT] + k, n_f) * per + i)

        specs, operands = [], []
        for (a0, a1), (g0, g1) in pairs:
            specs += [pl.BlockSpec((length, g_step), left)] * 2 + [fixed(length, g0.shape[1])] * 2
            operands += [a0, a1, g0, g1]
        if weights:
            for w, n in weights:
                if k == 0:
                    specs.append(pl.BlockSpec((g_step, n), lambda i, at: (i, at[J_AT])))
                else:
                    specs.append(pl.BlockSpec((g_step, n), lambda i, at: (i, 0)))
                operands.append(w)
            specs += [fixed(8, s.shape[1]) for s in sums]
            operands += list(sums)
        outs = [array((rows, n), f32 if k == 0 else bf16) for n in chunks]
        out_specs = [rows_of(g_step, n) for n in chunks]
        if weights:
            outs.append(array((rows, LANES), f32))
            out_specs.append(rows_of(g_step, LANES))
        return run(
            functools.partial(grads_kernel, len(pairs), len(weights), chunks),
            outs,
            (per,),
            specs,
            out_specs,
            operands,
            name=name,
        )

    y_rows = rows // n_y
    y_step = min(256, y_rows)
    y_per = y_rows // y_step

    def grads_y_kernel(at_ref, ins, outs, scratch):
        a0, a1, g0, g1 = ins[:4]
        weights, sums = ins[4 : 4 + n_f], ins[4 + n_f :]
        full = mm_tokens(a0[...], g0[...]) + mm_tokens(a1[...], g1[...])
        outs[0][...] = full.astype(outs[0].dtype)
        part_at = pl.program_id(0) // y_per
        w = weights[0][...].astype(f32)
        for q in range(1, n_f):
            w = jnp.where(part_at == q, weights[q][...].astype(f32), w)
        gain = jnp.sum(w * full, axis=1, keepdims=True)
        shift = jnp.sum(w * (sums[0][0:1] + sums[1][0:1]), axis=1, keepdims=True)
        lane = lax.broadcasted_iota(jnp.int32, (y_step, LANES), 1)
        outs[1][...] = jnp.where(lane == 0, gain, jnp.where(lane == 1, shift, 0.0))

    def grads_y(left, right, k, own_w, other_w, sums, name):
        n = right[0].shape[1]

        def offset(i, at):
            return rem(at[Y_AT] + k, n_y) * y_per + rem(i, y_per)

        def columns_at(i, at):
            return (0, rem(at[F_AT] + i // y_per, n_f) * (rows // y_step) + offset(i, at))

        weights = [own_w] + [other_w[n_f - q - 1] for q in range(1, n_f)]
        specs = [pl.BlockSpec((length, y_step), columns_at)] * 2 + [fixed(length, n)] * 2
        specs.append(pl.BlockSpec((y_step, n), lambda i, at: (offset(i, at), at[J_AT])))
        specs += [pl.BlockSpec((y_step, n), lambda i, at: (offset(i, at), 0))] * (n_f - 1)
        specs += [fixed(8, n)] * 2
        return run(
            grads_y_kernel,
            [array((n_f * y_rows, n), f32 if k == 0 else bf16), array((n_f * y_rows, LANES), f32)],
            (n_f * y_per,),
            specs,
            [rows_of(y_step, n), rows_of(y_step, LANES)],
            [*left, *right, *weights, *sums],
            name=name,
        )

    bufs = {}
    out_width = {"q": width, "k": width, "v": width, "o": width, "u": hidden, "d": hidden}

    def place_kernel(widths, at_ref, ins, outs, scratch):
        start = 0
        for out, w in zip(outs, widths):
            out[...] = ins[0][0, :, start : start + w].astype(f32)
            start += w

    def place(piece, y_from, crossed, targets):
        def out_spec(w, sub, subs):
            def index(i, at):
                core = (1 - at[C_AT]) if crossed else at[C_AT]
                return (rem(at[Y_AT] + n_y - y_from, n_y), (i * CORES + core) * subs + sub)

            return pl.BlockSpec((y_rows, w), index)

        names = [t[0] for t in targets]
        total = piece.shape[2]
        operands = [piece]
        aliases = {}
        for i, name in enumerate(names):
            if name in bufs:
                aliases[1 + len(operands)] = i
                operands.append(bufs[name])
        made = run(
            functools.partial(place_kernel, [t[1] for t in targets]),
            [array((rows, out_width[name]), f32) for name in names],
            (n_ctx,),
            [pl.BlockSpec((1, y_rows, total), lambda i, at: (i, 0, 0))] + [ANY] * (len(operands) - 1),
            [out_spec(*t[1:]) for t in targets],
            operands,
            aliases=aliases,
            name="place",
            limit=16,
        )
        for name, m in zip(names, made):
            bufs[name] = m

    def rsy(terms):
        return add(terms, bf16, "sum_pairs")

    def halves_kernel(at_ref, ins, outs, scratch):
        total = ins[0][...].astype(f32)
        for r in ins[1:]:
            total = total + r[...].astype(f32)
        for h in range(2):

            @pl.when(pl.program_id(0) == h)
            def _(h=h):
                outs[h][...] = total.astype(bf16)

    def rsy_halves(terms):
        n, w = terms[0].shape
        return run(
            halves_kernel,
            [array((n, w // 2), bf16)] * 2,
            (2,),
            [pl.BlockSpec((n, w // 2), lambda i, at: (0, i))] * len(terms),
            [fixed(n, w // 2)] * 2,
            terms,
            name="sum_pairs",
            limit=16,
        )

    def gather_z(piece):
        return lax.all_gather(piece, "ctx", axis=0, tiled=False)

    d_halves = [[("d", half_hid, h, 2)] for h in range(2)]
    qk_at = [("q", n_att, 0, 1), ("k", n_att, 0, 1)]
    vo_at = [("v", n_att, 0, 1), ("o", n_att, 0, 1)]

    first_in, second_in, act, slope, qkv = zip(forward(tok[0]), forward(tok[1]))
    att, lse = zip(attend(qkv[0]), attend(qkv[1]))
    mixed_other = core_swap(branch(act[1], att[1]))
    mixed_own = branch(act[0], att[0])
    mixed_terms = [to_owners(mixed_own, mixed_other, "sum_mixed")]
    pre0, do0, up_sum0 = down_back(cot[0], slope[0])
    down_sent = [grads([(cot, act)], [half_hid] * 2, k, [], [], "grad_down") for k in range(1, n_f)]
    down_got = [[over_f(p[0], k + 1) for k, p in enumerate(down_sent)]]
    down_own = grads([(cot, act)], [half_hid] * 2, 0, [], [], "grad_down")
    down_got.append([over_f(pin(p[1]), k + 1) for k, p in enumerate(down_sent)])
    pre1, do1, up_sum1 = down_back(cot[1], slope[1])
    pre, up_sums = (pre0, pre1), (up_sum0, up_sum1)

    def grads_up(k):
        return grads_y(second_in, pre, k, w_up, got_u, up_sums, "grad_up")

    def grads_att(k):
        return grads(
            [(first_in, dqkv), (cot, att)],
            [4 * n_att],
            k,
            [(w, n_att) for w in own_qkv] if k == 0 else [(got_qkv[n_f - k - 1], n_qkv)],
            qkv_sums,
            "grad_att",
        )

    def sent(parts):
        chunks = len(parts[0]) - 1
        return [[over_f(p[i], k + 1) for k, p in enumerate(parts)] for i in range(chunks)], [p[-1] for p in parts]

    def rsx(own, got):
        made = split_sum([own] + got, n_y, Y_AT, "sum_fsdp")
        return [made[0]] + [over_y(made[k], k) for k in range(1, n_y)]

    y_terms = [None] * 6
    z = [None] * 5
    targets = [d_halves[0], d_halves[1], [("u", n_hid, 0, 1)], qk_at, vo_at]
    def after_z(i, over=True):
        piece = pin(z[i])
        return piece, core_swap(piece), ([over_y(piece, k) for k in range(1, n_y)] if over else [])

    def after_y(pieces, after=()):
        pieces = [pin(p, after) for p in pieces]
        return [(p, core_swap(p)) for p in pieces]

    def place_own(i, piece, crossed, y_from=0):
        place(piece, y_from, False, targets[i])
        place(crossed, y_from, True, targets[i])

    def place_over(i, pieces):
        for k, (piece, crossed) in enumerate(pieces):
            place_own(i, piece, crossed, k + 1)

    o_step = min(64, block_rows)
    o_grid = (block_rows // o_step,)

    def mixed_kernel(at_ref, ins, outs, scratch):
        total = ins[0][...].astype(f32) + ins[1][0:1]
        for r in ins[2:]:
            total = total + r[...].astype(f32)
        outs[0][...] = total.astype(bf16)

    def make_mixed(mixed_terms):
        return run(
        mixed_kernel,
        [array((block_rows, width), bf16)],
        o_grid,
        [rows_of(o_step, width), fixed(8, width)] + [rows_of(o_step, width)] * len(mixed_terms),
        [rows_of(o_step, width)],
        [tokens[0], bias_last, *mixed_terms],
        name="mixed",
    )[0]

    def tokens_kernel(at_ref, ins, outs, scratch):
        g = ins[2][...].astype(f32)
        for r in ins[3:]:
            g = g + r[...].astype(f32)
        x = ins[0][...].astype(f32)
        center = x - jnp.mean(x, axis=-1, keepdims=True)
        inv = lax.rsqrt(jnp.mean(center * center, axis=-1, keepdims=True) + norm_eps)
        n = center * inv
        inner = g - jnp.mean(g, axis=-1, keepdims=True) - n * jnp.mean(g * n, axis=-1, keepdims=True)
        outs[0][...] = ins[1][...].astype(f32) + inv * inner

    def make_grad_tokens(back_terms):
        return run(
        tokens_kernel,
        [array((block_rows, width), f32)],
        o_grid,
        [rows_of(o_step, width)] * (2 + len(back_terms)),
        [rows_of(o_step, width)],
        [tokens[0], cotangent[0], *back_terms],
        name="grad_tokens",
    )[0]
    y_d0 = rsx(down_own[0], down_got[0])
    up_sent = [grads_up(k) for k in range(1, n_y)]
    up_got = [over_y(p[0], k + 1) for k, p in enumerate(up_sent)]
    z[0] = gather_z(rsy(y_d0))
    dqkv0, qkv_sum0 = attend_back(qkv[0], do0, lse[0])
    dqkv1, qkv_sum1 = attend_back(qkv[1], do1, lse[1])
    dqkv, qkv_sums = (dqkv0, dqkv1), (qkv_sum0, qkv_sum1)
    up_own = grads_up(0)
    dots_u = [up_own[1]] + [p[1] for p in up_sent]
    y_d1 = rsx(down_own[1], down_got[1])
    mixed = make_mixed(mixed_terms)
    att_own = grads_att(0)
    up_split = split_sum([up_own[0]] + up_got, n_f, None, "sum_fsdp")
    x_u = [up_split[0]] + [over_f(up_split[k], k) for k in range(1, n_f)]
    z[1] = gather_z(rsy(y_d1))
    p0, c0, o0 = after_z(0)
    att_got, att_dots = sent([grads_att(k) for k in range(1, n_f)])
    dots_a = [att_own[-1]] + att_dots
    def norm_grads(dots, gain, shift):
        ordered = dots[0] if n_f == 1 else None
        if n_f == 2:
            pair = jnp.stack([d[:, :2] for d in dots])
            ordered = jnp.stack([jnp.where(f_idx == m, pair[0], pair[1]) for m in range(2)])
        elif n_f > 2:
            ordered = jnp.roll(jnp.stack([d[:, :2] for d in dots]), f_idx, axis=0)
        ordered = ordered.reshape(width, -1)
        return (ordered[:, 0] - shift * ordered[:, 1]) / gain, ordered[:, 1]

    g_gain1, g_shift1 = norm_grads(dots_a, gain1, shift1)
    def by_rows(dots):
        cut = [d[:, :2].reshape(n_f, y_rows, 2) for d in dots]
        parts = [
            functools.reduce(lambda so_far, k: jnp.where(jnp.mod(m - y_idx, n_y) == k, cut[k], so_far), range(1, n_y), cut[0])
            for m in range(n_y)
        ]
        return list(jnp.stack(parts, axis=1).reshape(n_f, rows, 2))

    g_gain2, g_shift2 = norm_grads(by_rows(dots_u), gain2, shift2)
    qkv_sum = qkv_sum0[0] + qkv_sum1[0]
    up_sum = up_sum0[0] + up_sum1[0]

    def spot(vec, size):
        return lax.dynamic_update_slice_in_dim(jnp.zeros((size,), f32), vec, j_idx * vec.shape[0], axis=0)

    sums = [
        g_gain1,
        g_shift1,
        g_gain2,
        g_shift2,
        spot(qkv_sum[:n_att], width),
        spot(qkv_sum[n_att : n_att + ROT], heads * ROT),
        spot(qkv_sum[2 * n_att :], width),
        jnp.sum(cotangent[0].astype(f32), axis=0),
        spot(up_sum, hidden),
    ]
    vec = jnp.concatenate(sums).reshape(-1, LANES)

    vec = pin(vec)
    place_own(0, p0, c0)
    back_other = core_swap(back(dqkv[1], pre[1]))
    p1, c1, o1 = after_z(1)
    o0 = after_y(o0)
    z[2] = gather_z(rsy(x_u))
    place_own(1, p1, c1)
    place_over(0, o0)
    back_own = back(dqkv[0], pre[0])
    vec_f = [vec] + [over_f(vec, k) for k in range(1, n_f)]
    y_a = rsx(att_own[0], att_got[0])
    o1 = after_y(o1)
    vec = add(vec_f, f32, "sum_small")
    vec_c = [vec, core_swap(vec)]
    vec = add(vec_c, f32, "sum_small")
    vec_y = [vec] + [over_y(vec, k) for k in range(1, n_y)]
    vec = add(vec_y, f32, "sum_small")
    z[3], z[4] = [gather_z(p) for p in rsy_halves(y_a)]
    p2, c2, o2 = after_z(2)
    place_own(2, p2, c2)
    place_over(1, o1)
    back_terms = [to_owners(back_own, back_other, "sum_back")]
    o2 = after_y(o2)
    p3, c3, o3 = after_z(3)
    vec_z = [vec, lax.ppermute(vec, "ctx", [(0, 1), (1, 0), (2, 3), (3, 2)])]
    place_own(3, p3, c3)
    place_over(2, o2)
    vec = add(vec_z, f32, "sum_small")
    vec_z = [vec, lax.ppermute(vec, "ctx", [(0, 2), (2, 0), (1, 3), (3, 1)])]
    p4, c4, o4 = after_z(4)
    o3 = after_y(o3)
    place_own(4, p4, c4)
    place_over(3, o3)
    vec = add(vec_z, f32, "sum_small").reshape(-1)
    outs = []
    start = 0
    for s in sums:
        size = s.shape[0] // n_f
        outs.append(lax.dynamic_slice_in_dim(vec, start + f_idx * size, size, axis=0))
        start += s.shape[0]
    s_g1, s_b1, s_g2, s_b2, s_q, s_k, s_v, s_last, s_u = outs

    grad_tokens = make_grad_tokens(back_terms)
    o4 = after_y(o4, outs)
    place_over(4, o4)

    return (
        mixed[None],
        grad_tokens[None],
        s_g1,
        s_b1,
        s_g2,
        s_b2,
        bufs["q"],
        bufs["k"],
        bufs["v"],
        s_q,
        s_k,
        s_v,
        bufs["o"],
        s_last,
        bufs["u"],
        s_u,
        bufs["d"],
        s_last,
    )


def solution(mesh):
    seq = P(("dp", "fsdp"), "ctx", None)
    vec, mat = P("fsdp"), P("fsdp", None)
    params_in = (vec,) * 4 + (mat,) * 3 + (vec,) * 3 + (mat, vec, mat, vec, mat, vec)
    return jax.shard_map(
        functools.partial(local, mesh.shape["dp"], mesh.shape["ctx"], mesh.shape["fsdp"]),
        mesh=mesh,
        in_specs=(seq, seq) + params_in,
        out_specs=(seq, seq) + params_in,
        check_vma=False,
    )
```

time: 3670 us -> 651 us (0.18)
  waiting for transfers between devices: 3080 us -> 206 us
  Pallas kernels: 0 us -> 309 us
  matrix products: 253 us -> 0 us
  blocking collectives: 104 us -> 0 us
  other arithmetic: 103 us -> 8.64 us
    all_gather x8 -> x7, waiting for transfers between devices: 1230 us -> 32.6 us  [the longest x1 24 us: local(): own_tok = lax.all_gather(tokens[0], 'ctx', axis=0, tiled=True)]
    unnamed x13 -> x9, waiting for transfers between devices: 1090 us -> 0.81 us
    psum x1 -> x0, waiting for transfers between devices: 679 us -> none  [local(): lax.psum(fsdp_shard, ('dp', 'ctx')).astype(jnp.float32)]
    pallas_call x0 -> x76, Pallas kernels: none -> 309 us  [__call__(): pl.pallas_call(body, out_shape=tuple(outs) + (array((8, LANES), f32),), g...]
    dot_general x22 -> x0, matrix products: 248 us -> none  [the longest x6 65.1 us: rows_dot(): lax.dot_general(left, right, contract_rows, preferred_element_type=jnp.fl...]
    ppermute x0 -> x40, waiting for transfers between devices: none -> 165 us  [the longest x11 135 us: over_y(): return lax.ppermute(value, 'dp', shift_perm(n_dp, CORES * step))]
    reduce_scatter x2, waiting for transfers between devices: 79.4 us -> 8.03 us  [to_owners(): lax.psum_scatter(add([own, other_got], bf16, name), 'ctx', scatter_dimens...]
    concatenate x3 -> x11, other arithmetic: 69.2 us -> 4.58 us  [the longest x1 2.74 us: local(): jnp.concatenate([mine(w_down, n_hid), mine(w_out, n_att)], axis=1)]
  transfers between devices with their start and end apart: 12 -> 49, of which waited for: 12 -> 18; matrix products, arithmetic and copies ran while one was open for 7% -> 5% of each run, Pallas kernels for 0% -> 47%
where the time goes in v1:
time: 651 us; the launch traced here: 644 us
  Pallas kernels  309 us (47%)
  waiting for transfers between devices  206 us (32%)
  local copies, waits for them, and re-layouts  67.9 us (10%)
  starting transfers between devices  36.8 us (6%)
  between operations  15.3 us (2%)
  other arithmetic  8.64 us (1%)
    pallas_call x76, Pallas kernels, __call__(): pl.pallas_call(body, out_shape=tuple(outs) + (array((8, LANES), f32),), g...  309 us
    ppermute x11, waiting for transfers between devices, over_y(): return lax.ppermute(value, 'dp', shift_perm(n_dp, CORES * step))  135 us
    unnamed x166, local copies, waits for them, and re-layouts  48.8 us
    ppermute x9, waiting for transfers between devices, over_f(): return lax.ppermute(value, 'fsdp', shift_perm(n_f, step))  25.4 us
    all_gather x1, waiting for transfers between devices, local(): own_tok = lax.all_gather(tokens[0], 'ctx', axis=0, tiled=True)  24 us
    ppermute x18, starting transfers between devices, core_swap(): return lax.ppermute(value, 'dp', [(i, i ^ 1) for i in range(n_dp)])  13 us
  transfers between devices with their start and end apart: 49, of which 18 were waited for; matrix products, arithmetic and copies ran while one was open for 5% of the time, Pallas kernels for 47%

profile of v1, /device:TPU:1, one launch (start us, length us, event | category | flops | bytes accessed | tf_op | source)
XLA Modules:
  0.0 644.0 jit_solution(1813932004509080740)
XLA Ops:
  35.3 7.2 %collective-permute-done.1.refs_0_ = bf16[512,1024]{1,0:T(8,128)(2,1)} collective-permute-done((bf16[512,1024]{1,0:T(8,128)(2,1)}, bf16[512,1024]{1,0:T(8,128)(2,1)}, u32[]{:S(2)}, u32[]{:S(2)}) %collective-permute-start.1) | collective-permute-done | bytes 1048608 | tf_op jit(solution)/shard_map/ppermute | solution.py:173
  48.0 16.8 %collective-permute-done.2.refs_1_ = bf16[512,1024]{1,0:T(8,128)(2,1)} collective-permute-done((bf16[512,1024]{1,0:T(8,128)(2,1)}, bf16[512,1024]{1,0:T(8,128)(2,1)}, u32[]{:S(2)}, u32[]{:S(2)}) %collective-permute-start.2) | collective-permute-done | bytes 1048608 | tf_op jit(solution)/shard_map/ppermute | solution.py:167
  68.4 24.0 %all-gather.15.cloned.1.call-done = bf16[1,1024,2048]{2,1,0:T(8,128)(2,1)} async-done(((bf16[1,256,2048]{2,1,0:T(8,128)(2,1)}), bf16[1,1024,2048]{2,1,0:T(8,128)(2,1)}) %all-gather.15.cloned.1.call-update) | async-done | bytes 4194320 | tf_op jit(solution)/shard_map/all_gather | solution.py:184
  103.5 18.0 %forward.2 = (bf16[1024,2048]{1,0:T(8,128)(2,1)}, bf16[1024,2048]{1,0:T(8,128)(2,1)}, bf16[1024,1024]{1,0:T(8,128)(2,1)}, bf16[1024,1024]{1,0:T(8,128)(2,1)}, bf...) custom-call(s32[5]{0:T(128)S(1)} %stack.54.at_ref, bf16[1024,2048]{1,0:T(8,128)(2,1)} %copy-done.4, ...), custom_call_target="tpu_custom_call" | custom-call | flops 207000 | bytes 1 | tf_op jit(solution)/shard_map/forward/pallas_call | solution.py:83
  123.0 20.3 %forward.3 = (bf16[1024,2048]{1,0:T(8,128)(2,1)}, bf16[1024,2048]{1,0:T(8,128)(2,1)}, bf16[1024,1024]{1,0:T(8,128)(2,1)}, bf16[1024,1024]{1,0:T(8,128)(2,1)}, bf...) custom-call(s32[5]{0:T(128)S(1)} %stack.54.at_ref, bf16[256,2048]{1,0:T(8,128)(2,1)S(1)} %collective-permute-done.4.refs_0_, ...), custom_call_target="tpu_custom_call" | custom-call | flops 207000 | bytes 1 | tf_op jit(solution)/shard_map/forward/pallas_call | solution.py:83
  150.9 10.6 %branch.2 = (bf16[1024,2048]{1,0:T(8,128)(2,1)}, f32[8,128]{1,0:T(8,128)S(1)}) custom-call(s32[5]{0:T(128)S(1)} %stack.54.at_ref, bf16[1024,1024]{1,0:T(8,128)(2,1)S(1)} %copy-done.9, bf16[1024,256]{1,0:T(8,128)(2,1)S(1)} %get-tuple-element.230.refs_1_.refs_7_, bf16[1024,8192]{1,0:T(8,128)(2,1)} %refs_2_.7, bf16[1024,2048]{1,0:T(8,128)(2,1)} %refs_3_.9, ...), custom_call_target="tpu_custom_call" | custom-call | flops 115000 | bytes 1 | tf_op jit(solution)/shard_map/branch/pallas_call | solution.py:83
  161.6 10.4 %branch.3 = (bf16[1024,2048]{1,0:T(8,128)(2,1)}, f32[8,128]{1,0:T(8,128)S(1)}) custom-call(s32[5]{0:T(128)S(1)} %stack.54.at_ref, bf16[1024,1024]{1,0:T(8,128)(2,1)S(1)} %copy-done.8, bf16[1024,256]{1,0:T(8,128)(2,1)S(1)} %get-tuple-element.226.refs_1_.refs_6_, bf16[1024,8192]{1,0:T(8,128)(2,1)} %refs_2_.7, bf16[1024,2048]{1,0:T(8,128)(2,1)} %refs_3_.9, ...), custom_call_target="tpu_custom_call" | custom-call | flops 115000 | bytes 1 | tf_op jit(solution)/shard_map/branch/pallas_call | solution.py:83
  178.4 9.9 %down_back.2 = (bf16[1024,1024]{1,0:T(8,128)(2,1)S(1)}, bf16[1024,256]{1,0:T(8,128)(2,1)S(1)}, f32[8,1024]{1,0:T(8,128)S(1)}, f32[8,128]{1,0:T(8,128)S(1)}) custom-call(s32[5]{0:T(128)S(1)} %stack.54.at_ref, bf16[1024,2048]{1,0:T(8,128)(2,1)} %bitcast.61, bf16[1024,1024]{1,0:T(8,128)(2,1)} %get-tuple-element.237.refs_1_, bf16[1024,8192]{1,0:T(8,128)(2,1)} %refs_2_.7, ...), custom_call_target="tpu_custom_call" | custom-call | flops 115000 | bytes 1 | tf_op jit(solution)/shard_map/down_back/pallas_call | solution.py:83
  192.4 8.4 %grad_down.2 = (bf16[1024,512]{1,0:T(8,128)(2,1)S(1)}, bf16[1024,512]{1,0:T(8,128)(2,1)S(1)}, f32[8,128]{1,0:T(8,128)S(1)}) custom-call(s32[5]{0:T(128)S(1)} %stack.54.at_ref, bf16[1024,2048]{1,0:T(8,128)(2,1)} %bitcast.62, bf16[1024,2048]{1,0:T(8,128)(2,1)} %copy-done.64, bf16[1024,1024]{1,0:T(8,128)(2,1)} %get-tuple-element.222.refs_0_.refs_2_, ...), custom_call_target="tpu_custom_call" | custom-call | flops 103500 | bytes 1 | tf_op jit(solution)/shard_map/grad_down/pallas_call | solution.py:83
  202.1 9.2 %grad_down.3 = (f32[1024,512]{1,0:T(8,128)S(1)}, f32[1024,512]{1,0:T(8,128)}, f32[8,128]{1,0:T(8,128)S(1)}) custom-call(s32[5]{0:T(128)S(1)} %stack.54.at_ref, bf16[1024,2048]{1,0:T(8,128)(2,1)} %bitcast.63, bf16[1024,2048]{1,0:T(8,128)(2,1)} %copy-done.64, bf16[1024,1024]{1,0:T(8,128)(2,1)} %get-tuple-element.222.refs_0_.refs_2_, ...), custom_call_target="tpu_custom_call" | custom-call | flops 103500 | bytes 1 | tf_op jit(solution)/shard_map/grad_down/pallas_call | solution.py:83
  212.8 9.9 %down_back.3 = (bf16[1024,1024]{1,0:T(8,128)(2,1)S(1)}, bf16[1024,256]{1,0:T(8,128)(2,1)S(1)}, f32[8,1024]{1,0:T(8,128)S(1)}, f32[8,128]{1,0:T(8,128)S(1)}) custom-call(s32[5]{0:T(128)S(1)} %stack.54.at_ref, bf16[1024,2048]{1,0:T(8,128)(2,1)} %copy-done.64, bf16[1024,1024]{1,0:T(8,128)(2,1)} %get-tuple-element.248.refs_1_, bf16[1024,8192]{1,0:T(8,128)(2,1)} %refs_2_.7, ...), custom_call_target="tpu_custom_call" | custom-call | flops 115000 | bytes 1 | tf_op jit(solution)/shard_map/down_back/pallas_call | solution.py:83
  227.7 9.5 %grad_up.2 = (bf16[1024,1024]{1,0:T(8,128)(2,1)S(1)}, f32[1024,128]{1,0:T(8,128)S(1)}, f32[8,128]{1,0:T(8,128)S(1)}) custom-call(s32[5]{0:T(128)S(1)} %stack.54.at_ref, bf16[1024,2048]{1,0:T(8,128)(2,1)} %get-tuple-element.245.refs_0_, bf16[1024,2048]{1,0:T(8,128)(2,1)} %get-tuple-element.246.refs_1_, bf16[1024,1024]{1,0:T(8,128)(2,1)} %copy-done.5, ...), custom_call_target="tpu_custom_call" | custom-call | flops 103500 | bytes 1 | tf_op jit(solution)/shard_map/grad_up/pallas_call | solution.py:83
  259.1 10.2 %grad_up.3 = (f32[1024,1024]{1,0:T(8,128)}, f32[1024,128]{1,0:T(8,128)S(1)}, f32[8,128]{1,0:T(8,128)S(1)}) custom-call(s32[5]{0:T(128)S(1)} %stack.54.at_ref, bf16[1024,2048]{1,0:T(8,128)(2,1)} %get-tuple-element.245.refs_0_, bf16[1024,2048]{1,0:T(8,128)(2,1)} %get-tuple-element.246.refs_1_, bf16[1024,1024]{1,0:T(8,128)(2,1)S(1)} %copy-done.6, ...), custom_call_target="tpu_custom_call" | custom-call | flops 103500 | bytes 1 | tf_op jit(solution)/shard_map/grad_up/pallas_call | solution.py:83
  281.9 10.6 %grad_att.2 = (f32[1024,1024]{1,0:T(8,128)}, f32[1024,128]{1,0:T(8,128)S(1)}, f32[8,128]{1,0:T(8,128)S(1)}) custom-call(s32[5]{0:T(128)S(1)} %stack.54.at_ref, bf16[1024,2048]{1,0:T(8,128)(2,1)} %get-tuple-element.276.refs_0_, bf16[1024,2048]{1,0:T(8,128)(2,1)} %get-tuple-element.277.refs_1_, bf16[1024,768]{1,0:T(8,128)(2,1)S(1)} %copy-done.10, ...), custom_call_target="tpu_custom_call" | custom-call | flops 103500 | bytes 1 | tf_op jit(solution)/shard_map/grad_att/pallas_call | solution.py:83
  306.1 9.9 %grad_att.3 = (bf16[1024,1024]{1,0:T(8,128)(2,1)}, f32[1024,128]{1,0:T(8,128)S(1)}, f32[8,128]{1,0:T(8,128)S(1)}) custom-call(s32[5]{0:T(128)S(1)} %stack.54.at_ref, bf16[1024,2048]{1,0:T(8,128)(2,1)} %get-tuple-element.276.refs_0_, bf16[1024,2048]{1,0:T(8,128)(2,1)} %get-tuple-element.277.refs_1_, bf16[1024,768]{1,0:T(8,128)(2,1)S(1)} %copy-done.10, ...), custom_call_target="tpu_custom_call" | custom-call | flops 103500 | bytes 1 | tf_op jit(solution)/shard_map/grad_att/pallas_call | solution.py:83
  328.3 13.0 %back.2 = (bf16[1024,2048]{1,0:T(8,128)(2,1)}, f32[8,128]{1,0:T(8,128)S(1)}) custom-call(s32[5]{0:T(128)S(1)} %stack.54.at_ref, bf16[1024,768]{1,0:T(8,128)(2,1)S(1)} %copy-done.11, bf16[1024,1024]{1,0:T(8,128)(2,1)} %copy-done.7, f32[8,2048]{1,0:T(8,128)S(1)} %get-tuple-element.214.refs_1_.refs_4_.refs_2_, bf16[1024,2048]{1,0:T(8,128)(2,1)} %refs_3_.11, ...), custom_call_target="tpu_custom_call" | custom-call | flops 149500 | bytes 1 | tf_op jit(solution)/shard_map/back/pallas_call | solution.py:83
  341.3 6.7 %all-gather.21.cloned.1.call-done = bf16[2048,512]{1,0:T(8,128)(2,1)} async-done(((bf16[512,512]{1,0:T(8,128)(2,1)}), bf16[2048,512]{1,0:T(8,128)(2,1)}) %all-gather.21.cloned.1.call-update) | async-done | bytes 2097168 | tf_op jit(solution)/shard_map/all_gather | solution.py:707
  373.7 13.3 %back.3 = (bf16[1024,2048]{1,0:T(8,128)(2,1)}, f32[8,128]{1,0:T(8,128)S(1)}) custom-call(s32[5]{0:T(128)S(1)} %stack.54.at_ref, bf16[1024,768]{1,0:T(8,128)(2,1)S(1)} %copy-done.10, bf16[1024,1024]{1,0:T(8,128)(2,1)} %copy-done.5, f32[8,2048]{1,0:T(8,128)S(1)} %get-tuple-element.214.refs_1_.refs_4_.refs_2_, bf16[1024,2048]{1,0:T(8,128)(2,1)} %refs_3_.11, ...), custom_call_target="tpu_custom_call" | custom-call | flops 149500 | bytes 1 | tf_op jit(solution)/shard_map/back/pallas_call | solution.py:83
  387.0 16.1 %collective-permute-done.23.refs_1_ = bf16[1024,1024]{1,0:T(8,128)(2,1)S(1)} collective-permute-done((bf16[1024,1024]{1,0:T(8,128)(2,1)}, bf16[1024,1024]{1,0:T(8,128)(2,1)S(1)}, u32[]{:S(2)}, u32[]{:S(2)}) %collective-permute-start.23) | collective-permute-done | bytes 2097184 | tf_op jit(solution)/shard_map/ppermute | solution.py:173
  413.9 15.9 %collective-permute-done.28.refs_1_ = f32[180,128]{1,0:T(8,128)S(1)} collective-permute-done((f32[180,128]{1,0:T(8,128)S(1)}, f32[180,128]{1,0:T(8,128)S(1)}, u32[]{:S(2)}, u32[]{:S(2)}) %collective-permute-start.28) | collective-permute-done | bytes 92192 | tf_op jit(solution)/shard_map/ppermute | solution.py:167
  463.6 64.9 %collective-permute-done.31.refs_0_ = bf16[4,512,1024]{2,1,0:T(8,128)(2,1)} collective-permute-done((bf16[4,512,1024]{2,1,0:T(8,128)(2,1)}, bf16[4,512,1024]{2,1,0:T(8,128)(2,1)}, u32[]{:S(2)}, u32[]{:S(2)}) %collective-permute-start.31) | collective-permute-done | bytes 4194336 | tf_op jit(solution)/shard_map/ppermute | solution.py:167
  558.0 20.2 %collective-permute-done.35.refs_0_ = bf16[4,512,512]{2,1,0:T(8,128)(2,1)S(1)} collective-permute-done((bf16[4,512,512]{2,1,0:T(8,128)(2,1)}, bf16[4,512,512]{2,1,0:T(8,128)(2,1)S(1)}, u32[]{:S(2)}, u32[]{:S(2)}) %collective-permute-start.35) | collective-permute-done | bytes 2097184 | tf_op jit(solution)/shard_map/ppermute | solution.py:167
  599.8 8.0 %reduce-scatter.5.cloned.1.call-done.refs_2_ = bf16[256,2048]{1,0:T(8,128)(2,1)} async-done(((bf16[1024,2048]{1,0:T(8,128)(2,1)}), bf16[256,2048]{1,0:T(8,128)(2,1)}) %reduce-scatter.5.cloned.1.call-update) | async-done | bytes 1048592 | tf_op jit(solution)/shard_map/reduce_scatter | solution.py:476
  612.5 15.0 %collective-permute-done.38.refs_0_ = bf16[4,512,512]{2,1,0:T(8,128)(2,1)} collective-permute-done((bf16[4,512,512]{2,1,0:T(8,128)(2,1)}, bf16[4,512,512]{2,1,0:T(8,128)(2,1)}, u32[]{:S(2)}, u32[]{:S(2)}) %collective-permute-start.38) | collective-permute-done | bytes 2097184 | tf_op jit(solution)/shard_map/ppermute | solution.py:167
  (391 shorter events, 270.6 us)
Async XLA Ops:
  7.2 85.3 %all-gather.15.cloned.1.call-start = ((), (), s32[]{:S(2)}) async-start(), calls=%async_computation.4 | async-start | bytes 5242880 | tf_op jit(solution)/shard_map/all_gather | solution.py:184
  7.9 169.9 %all-gather.17.cloned.1.call-start = ((), (), s32[]{:S(2)}) async-start(), calls=%async_computation.5 | async-start | bytes 5242880 | tf_op jit(solution)/shard_map/all_gather | solution.py:185
  22.3 80.0 %collective-permute-start.3 = (bf16[1024,768]{1,0:T(8,128)(2,1)}, bf16[1024,768]{1,0:T(8,128)(2,1)S(1)}, u32[]{:S(2)}, u32[]{:S(2)}) collective-permute-start(bf16[1024,768]{1,0:T(8,128)(2,1)} %pad_maximum_fusion.1), channel_id=1, source_target_pairs={{0,1},{1,0},{2,3},{3,2},{4,5},{5,4},{6,7},{7,6},{8,9},{9,8},{10,11... | collective-permute-start | bytes 4718600 | tf_op jit(solution)/shard_map/ppermute | solution.py:173
  47.1 103.8 %collective-permute-start.8 = (bf16[1024,1280]{1,0:T(8,128)(2,1)}, bf16[1024,1280]{1,0:T(8,128)(2,1)}, u32[]{:S(2)}, u32[]{:S(2)}) collective-permute-start(bf16[1024,1280]{1,0:T(8,128)(2,1)} %pad_maximum_fusion), channel_id=1, source_target_pairs={{0,1},{1,0},{2,3},{3,2},{4,5},{5,4},{6,7},{7,6},{8,9},{9,8},{10,11... | collective-permute-start | bytes 7864328 | tf_op jit(solution)/shard_map/ppermute | solution.py:173
  47.4 229.9 %reduce-scatter.3.cloned.1.call-start = ((), (), s32[]{:S(2)}) async-start(), calls=%async_computation.2 | async-start | bytes 5242880 | tf_op jit(solution)/shard_map/reduce_scatter | solution.py:476
  177.7 123.5 %all-gather.19.cloned.1.call-start = ((), (), s32[]{:S(2)}) async-start(), calls=%async_computation.6 | async-start | bytes 2621440 | tf_op jit(solution)/shard_map/all_gather | solution.py:707
  200.7 24.9 %collective-permute-start.12 = (bf16[1024,512]{1,0:T(8,128)(2,1)S(1)}, bf16[1024,512]{1,0:T(8,128)(2,1)S(1)}, u32[]{:S(2)}, u32[]{:S(2)}) collective-permute-start(bf16[1024,512]{1,0:T(8,128)(2,1)S(1)} %get-tuple-element.258), channel_id=1, source_target_pairs={{0,1},{1,0},{2,3},{3,2},{4,5},{5,4},{6,7},{7,6},{8,9},{9,8},{10,11... | collective-permute-start | bytes 3145736 | tf_op jit(solution)/shard_map/ppermute | solution.py:173
  241.0 107.1 %all-gather.21.cloned.1.call-start = ((), (), s32[]{:S(2)}) async-start(), calls=%async_computation.7 | async-start | bytes 2621440 | tf_op jit(solution)/shard_map/all_gather | solution.py:707
  241.2 51.3 %collective-permute-start.15 = (bf16[1024,1024]{1,0:T(8,128)(2,1)}, bf16[1024,1024]{1,0:T(8,128)(2,1)}, u32[]{:S(2)}, u32[]{:S(2)}) collective-permute-start(bf16[1024,1024]{1,0:T(8,128)(2,1)} %copy-done.62), channel_id=1, source_target_pairs={{0,16},{8,24},{16,0},{24,8},{1,17},{9,25},{17,1},{25,9},{2,18},{10... | collective-permute-start | bytes 6291464 | tf_op jit(solution)/shard_map/ppermute | solution.py:167
  242.3 27.0 %collective-permute-start.11 = (bf16[1024,512]{1,0:T(8,128)(2,1)}, bf16[1024,512]{1,0:T(8,128)(2,1)}, u32[]{:S(2)}, u32[]{:S(2)}) collective-permute-start(bf16[1024,512]{1,0:T(8,128)(2,1)} %copy-done.39), channel_id=1, source_target_pairs={{0,1},{1,0},{2,3},{3,2},{4,5},{5,4},{6,7},{7,6},{8,9},{9,8},{10,11... | collective-permute-start | bytes 3145736 | tf_op jit(solution)/shard_map/ppermute | solution.py:173
  273.2 25.3 %collective-permute-start.14 = (bf16[512,512]{1,0:T(8,128)(2,1)}, bf16[512,512]{1,0:T(8,128)(2,1)}, u32[]{:S(2)}, u32[]{:S(2)}) collective-permute-start(bf16[512,512]{1,0:T(8,128)(2,1)} %get-tuple-element.273), channel_id=1, source_target_pairs={{0,16},{8,24},{16,0},{24,8},{1,17},{9,25},{17,1},{25,9},{2,18},{10... | collective-permute-start | bytes 1572872 | tf_op jit(solution)/shard_map/ppermute | solution.py:167
  300.9 134.0 %all-gather.23.cloned.1.call-start = ((), (), s32[]{:S(2)}) async-start(), calls=%async_computation.8 | async-start | bytes 5242880 | tf_op jit(solution)/shard_map/all_gather | solution.py:707
  304.0 47.5 %collective-permute-start.16 = (bf16[4,512,512]{2,1,0:T(8,128)(2,1)}, bf16[4,512,512]{2,1,0:T(8,128)(2,1)}, u32[]{:S(2)}, u32[]{:S(2)}) collective-permute-start(bf16[4,512,512]{2,1,0:T(8,128)(2,1)} %get-tuple-element.285.refs_0_), channel_id=1, source_target_pairs={{0,16},{8,24},{16,0},{24,8},{1,17},{9,25},{17,1},{25,9},{2,18},{10... | collective-permute-start | bytes 6291464 | tf_op jit(solution)/shard_map/ppermute | solution.py:167
  316.4 35.6 %collective-permute-start.20 = (bf16[512,1024]{1,0:T(8,128)(2,1)}, bf16[512,1024]{1,0:T(8,128)(2,1)}, u32[]{:S(2)}, u32[]{:S(2)}) collective-permute-start(bf16[512,1024]{1,0:T(8,128)(2,1)} %copy-done.63), channel_id=1, source_target_pairs={{0,1},{1,0},{2,3},{3,2},{4,5},{5,4},{6,7},{7,6},{8,9},{9,8},{10,11... | collective-permute-start | bytes 3145736 | tf_op jit(solution)/shard_map/ppermute | solution.py:173
  354.9 175.5 %all-gather.25.cloned.1.call-start = ((), (), s32[]{:S(2)}) async-start(), calls=%async_computation.9 | async-start | bytes 2621440 | tf_op jit(solution)/shard_map/all_gather | solution.py:707
  356.0 47.1 %collective-permute-start.23 = (bf16[1024,1024]{1,0:T(8,128)(2,1)}, bf16[1024,1024]{1,0:T(8,128)(2,1)S(1)}, u32[]{:S(2)}, u32[]{:S(2)}) collective-permute-start(bf16[1024,1024]{1,0:T(8,128)(2,1)} %get-tuple-element.316), channel_id=1, source_target_pairs={{0,1},{1,0},{2,3},{3,2},{4,5},{5,4},{6,7},{7,6},{8,9},{9,8},{10,11... | collective-permute-start | bytes 6291464 | tf_op jit(solution)/shard_map/ppermute | solution.py:173
  357.2 49.4 %collective-permute-start.22 = (bf16[4,512,512]{2,1,0:T(8,128)(2,1)}, bf16[4,512,512]{2,1,0:T(8,128)(2,1)S(1)}, u32[]{:S(2)}, u32[]{:S(2)}) collective-permute-start(bf16[4,512,512]{2,1,0:T(8,128)(2,1)} %copy-done.17), channel_id=1, source_target_pairs={{0,16},{8,24},{16,0},{24,8},{1,17},{9,25},{17,1},{25,9},{2,18},{10... | collective-permute-start | bytes 6291464 | tf_op jit(solution)/shard_map/ppermute | solution.py:167
  404.1 26.2 %collective-permute-start.25 = (bf16[512,1024]{1,0:T(8,128)(2,1)S(1)}, bf16[512,1024]{1,0:T(8,128)(2,1)S(1)}, u32[]{:S(2)}, u32[]{:S(2)}) collective-permute-start(bf16[512,1024]{1,0:T(8,128)(2,1)S(1)} %get-tuple-element.323), channel_id=1, source_target_pairs={{0,16},{8,24},{16,0},{24,8},{1,17},{9,25},{17,1},{25,9},{2,18},{10... | collective-permute-start | bytes 3145736 | tf_op jit(solution)/shard_map/ppermute | solution.py:167
  433.2 123.7 %all-gather.27.cloned.1.call-start = ((), (), s32[]{:S(2)}) async-start(), calls=%async_computation.10 | async-start | bytes 2621440 | tf_op jit(solution)/shard_map/all_gather | solution.py:707
  436.2 171.6 %reduce-scatter.5.cloned.1.call-start = ((), (), s32[]{:S(2)}) async-start(), calls=%async_computation.3 | async-start | bytes 5242880 | tf_op jit(solution)/shard_map/reduce_scatter | solution.py:476
  436.4 92.1 %collective-permute-start.31 = (bf16[4,512,1024]{2,1,0:T(8,128)(2,1)}, bf16[4,512,1024]{2,1,0:T(8,128)(2,1)}, u32[]{:S(2)}, u32[]{:S(2)}) collective-permute-start(bf16[4,512,1024]{2,1,0:T(8,128)(2,1)} %get-tuple-element.332.refs_0_), channel_id=1, source_target_pairs={{0,16},{8,24},{16,0},{24,8},{1,17},{9,25},{17,1},{25,9},{2,18},{10... | collective-permute-start | bytes 12582920 | tf_op jit(solution)/shard_map/ppermute | solution.py:167
  531.1 47.1 %collective-permute-start.35 = (bf16[4,512,512]{2,1,0:T(8,128)(2,1)}, bf16[4,512,512]{2,1,0:T(8,128)(2,1)S(1)}, u32[]{:S(2)}, u32[]{:S(2)}) collective-permute-start(bf16[4,512,512]{2,1,0:T(8,128)(2,1)} %get-tuple-element.347.refs_0_), channel_id=1, source_target_pairs={{0,16},{8,24},{16,0},{24,8},{1,17},{9,25},{17,1},{25,9},{2,18},{10... | collective-permute-start | bytes 6291464 | tf_op jit(solution)/shard_map/ppermute | solution.py:167
  557.5 29.0 %collective-permute-start.37 = (bf16[4,512,512]{2,1,0:T(8,128)(2,1)}, bf16[4,512,512]{2,1,0:T(8,128)(2,1)}, u32[]{:S(2)}, u32[]{:S(2)}) collective-permute-start(bf16[4,512,512]{2,1,0:T(8,128)(2,1)} %get-tuple-element.363.refs_0_), channel_id=1, source_target_pairs={{0,8},{8,0},{16,24},{24,16},{1,9},{9,1},{17,25},{25,17},{2,10},{10... | collective-permute-start | bytes 6291464 | tf_op jit(solution)/shard_map/ppermute | solution.py:164
  580.0 47.5 %collective-permute-start.38 = (bf16[4,512,512]{2,1,0:T(8,128)(2,1)}, bf16[4,512,512]{2,1,0:T(8,128)(2,1)}, u32[]{:S(2)}, u32[]{:S(2)}) collective-permute-start(bf16[4,512,512]{2,1,0:T(8,128)(2,1)} %get-tuple-element.363.refs_0_), channel_id=1, source_target_pairs={{0,16},{8,24},{16,0},{24,8},{1,17},{9,25},{17,1},{25,9},{2,18},{10... | collective-permute-start | bytes 6291464 | tf_op jit(solution)/shard_map/ppermute | solution.py:167
  (101 other events, 1047.9 us)
Sparse Core Ops, SparseCore 0:
  9.6 82.8 all-gather.14
  94.0 79.2 all-gather.16
  177.9 75.2 reduce-scatter.2
  254.7 46.4 all-gather.18
  303.3 44.7 all-gather.20
  355.1 79.7 all-gather.22
  437.1 44.4 all-gather.24
  483.2 44.6 all-gather.26
  530.3 77.5 reduce-scatter.4

commit v2 on v1

--- a/solution.py
+++ b/solution.py
@@ -63,6 +63,7 @@
     "place": 4,
     "mixed": 3,
     "grad_tokens": 4,
+    "stack": 2,
 }
 
 
@@ -644,19 +645,23 @@
     def place_kernel(widths, at_ref, ins, outs, scratch):
         start = 0
         for out, w in zip(outs, widths):
-            out[...] = ins[0][0, :, start : start + w].astype(f32)
+            out[...] = ins[0][0, 0, :, start : start + w].astype(f32)
             start += w
 
     def place(piece, y_from, crossed, targets):
+        if piece.ndim == 3:
+            piece = piece[:, None]
+        stacked = piece.shape[1]
+
         def out_spec(w, sub, subs):
-            def index(i, at):
+            def index(i, j, at):
                 core = (1 - at[C_AT]) if crossed else at[C_AT]
-                return (rem(at[Y_AT] + n_y - y_from, n_y), (i * CORES + core) * subs + sub)
+                return (rem(at[Y_AT] + 2 * n_y - y_from - j, n_y), (i * CORES + core) * subs + sub)
 
             return pl.BlockSpec((y_rows, w), index)
 
         names = [t[0] for t in targets]
-        total = piece.shape[2]
+        total = piece.shape[3]
         operands = [piece]
         aliases = {}
         for i, name in enumerate(names):
@@ -666,13 +671,13 @@
         made = run(
             functools.partial(place_kernel, [t[1] for t in targets]),
             [array((rows, out_width[name]), f32) for name in names],
-            (n_ctx,),
-            [pl.BlockSpec((1, y_rows, total), lambda i, at: (i, 0, 0))] + [ANY] * (len(operands) - 1),
+            (n_ctx, stacked),
+            [pl.BlockSpec((1, 1, y_rows, total), lambda i, j, at: (i, j, 0, 0))] + [ANY] * (len(operands) - 1),
             [out_spec(*t[1:]) for t in targets],
             operands,
             aliases=aliases,
             name="place",
-            limit=16,
+            limit=20,
         )
         for name, m in zip(names, made):
             bufs[name] = m
@@ -680,35 +685,61 @@
     def rsy(terms):
         return add(terms, bf16, "sum_pairs")
 
-    def halves_kernel(at_ref, ins, outs, scratch):
+    def cut_kernel(first, at_ref, ins, outs, scratch):
         total = ins[0][...].astype(f32)
         for r in ins[1:]:
             total = total + r[...].astype(f32)
-        for h in range(2):
-
-            @pl.when(pl.program_id(0) == h)
-            def _(h=h):
-                outs[h][...] = total.astype(bf16)
-
-    def rsy_halves(terms):
-        n, w = terms[0].shape
-        return run(
-            halves_kernel,
-            [array((n, w // 2), bf16)] * 2,
-            (2,),
-            [pl.BlockSpec((n, w // 2), lambda i, at: (0, i))] * len(terms),
-            [fixed(n, w // 2)] * 2,
+
+        @pl.when(pl.program_id(0) < first)
+        def _():
+            outs[0][...] = total.astype(bf16)
+
+        @pl.when(pl.program_id(0) >= first)
+        def _():
+            outs[1][...] = total.astype(bf16)
+
+    def rsy_cut(terms, w):
+        n, all_w = terms[0].shape
+        first = all_w // w - 1
+        return run(
+            functools.partial(cut_kernel, first),
+            [array((n, first * w), bf16), array((n, w), bf16)],
+            (first + 1,),
+            [pl.BlockSpec((n, w), lambda i, at: (0, i))] * len(terms),
+            [
+                pl.BlockSpec((n, w), lambda i, at: (0, jnp.minimum(i, first - 1))),
+                pl.BlockSpec((n, w), lambda i, at: (0, 0)),
+            ],
             terms,
             name="sum_pairs",
             limit=16,
         )
 
+    def stack_kernel(at_ref, ins, outs, scratch):
+        for m, r in enumerate(ins):
+
+            @pl.when(pl.program_id(0) == m)
+            def _(r=r):
+                outs[0][0] = r[...]
+
+    def stack(pieces):
+        n, w = pieces[0].shape
+        return run(
+            stack_kernel,
+            [array((len(pieces), n, w), bf16)],
+            (len(pieces),),
+            [fixed(n, w)] * len(pieces),
+            [pl.BlockSpec((1, n, w), lambda i, at: (i, 0, 0))],
+            pieces,
+            name="stack",
+            limit=16,
+        )[0]
+
     def gather_z(piece):
         return lax.all_gather(piece, "ctx", axis=0, tiled=False)
 
     d_halves = [[("d", half_hid, h, 2)] for h in range(2)]
-    qk_at = [("q", n_att, 0, 1), ("k", n_att, 0, 1)]
-    vo_at = [("v", n_att, 0, 1), ("o", n_att, 0, 1)]
+    qkv_at = [(name, n_att, 0, 1) for name in ("q", "k", "v")]
 
     first_in, second_in, act, slope, qkv = zip(forward(tok[0]), forward(tok[1]))
     att, lse = zip(attend(qkv[0]), attend(qkv[1]))
@@ -746,7 +777,7 @@
 
     y_terms = [None] * 6
     z = [None] * 5
-    targets = [d_halves[0], d_halves[1], [("u", n_hid, 0, 1)], qk_at, vo_at]
+    targets = [d_halves[0], d_halves[1], [("u", n_hid, 0, 1)], qkv_at, [("o", n_att, 0, 1)]]
     def after_z(i, over=True):
         piece = pin(z[i])
         return piece, core_swap(piece), ([over_y(piece, k) for k in range(1, n_y)] if over else [])
@@ -878,7 +909,9 @@
     vec = add(vec_c, f32, "sum_small")
     vec_y = [vec] + [over_y(vec, k) for k in range(1, n_y)]
     vec = add(vec_y, f32, "sum_small")
-    z[3], z[4] = [gather_z(p) for p in rsy_halves(y_a)]
+    qkv_piece, o_piece = rsy_cut(y_a, n_att)
+    z[3] = gather_z(qkv_piece)
+    z[4] = gather_z(stack([o_piece] + [over_y(o_piece, k) for k in range(1, n_y)]))
     p2, c2, o2 = after_z(2)
     place_own(2, p2, c2)
     place_over(1, o1)
@@ -889,11 +922,9 @@
     place_own(3, p3, c3)
     place_over(2, o2)
     vec = add(vec_z, f32, "sum_small")
+    p4, c4, _ = after_z(4, False)
     vec_z = [vec, lax.ppermute(vec, "ctx", [(0, 2), (2, 0), (1, 3), (3, 1)])]
-    p4, c4, o4 = after_z(4)
-    o3 = after_y(o3)
     place_own(4, p4, c4)
-    place_over(3, o3)
     vec = add(vec_z, f32, "sum_small").reshape(-1)
     outs = []
     start = 0
@@ -903,9 +934,12 @@
         start += s.shape[0]
     s_g1, s_b1, s_g2, s_b2, s_q, s_k, s_v, s_last, s_u = outs
 
+    o3 = after_y(o3, outs)
+    for k, (piece, _) in enumerate(o3):
+        place(piece, k + 1, False, targets[3])
     grad_tokens = make_grad_tokens(back_terms)
-    o4 = after_y(o4, outs)
-    place_over(4, o4)
+    for k, (_, crossed) in enumerate(o3):
+        place(crossed, k + 1, True, targets[3])
 
     return (
         mixed[None],

time: 651 us -> 655 us (level)
    ppermute x11, waiting for transfers between devices: 135 us -> 126 us  [over_y(): return lax.ppermute(value, 'dp', shift_perm(n_dp, CORES * step))]
    pallas_call x76 -> x74, Pallas kernels: 309 us -> 312 us  [__call__(): pl.pallas_call(body, out_shape=tuple(outs) + (array((8, LANES), f32),), g...]
    ppermute x18 -> x17, starting transfers between devices: 13 us -> 14.3 us  [core_swap(): return lax.ppermute(value, 'dp', [(i, i ^ 1) for i in range(n_dp)])]
  transfers between devices with their start and end apart: 49 -> 48, of which waited for: 18 -> 17; matrix products, arithmetic and copies ran while one was open for 5% -> 5% of each run, Pallas kernels for 47% -> 47%
where the time goes in v2:
time: 655 us; the launch traced here: 647 us
  Pallas kernels  312 us (48%)
  waiting for transfers between devices  203 us (31%)
  local copies, waits for them, and re-layouts  69.6 us (11%)
  starting transfers between devices  38.4 us (6%)
  between operations  15.2 us (2%)
  other arithmetic  8.64 us (1%)
    pallas_call x74, Pallas kernels, __call__(): pl.pallas_call(body, out_shape=tuple(outs) + (array((8, LANES), f32),), g...  312 us
    ppermute x11, waiting for transfers between devices, over_y(): return lax.ppermute(value, 'dp', shift_perm(n_dp, CORES * step))  126 us
    unnamed x166, local copies, waits for them, and re-layouts  50.6 us
    ppermute x9, waiting for transfers between devices, over_f(): return lax.ppermute(value, 'fsdp', shift_perm(n_f, step))  25.4 us
    all_gather x1, waiting for transfers between devices, local(): own_tok = lax.all_gather(tokens[0], 'ctx', axis=0, tiled=True)  24 us
    ppermute x17, starting transfers between devices, core_swap(): return lax.ppermute(value, 'dp', [(i, i ^ 1) for i in range(n_dp)])  14.3 us
    reduce_scatter x2, waiting for transfers between devices, to_owners(): lax.psum_scatter(add([own, other_got], bf16, name), 'ctx', scatter_dimens...  14.2 us
  transfers between devices with their start and end apart: 48, of which 17 were waited for; matrix products, arithmetic and copies ran while one was open for 5% of the time, Pallas kernels for 47%

profile of v2, /device:TPU:1, one launch (start us, length us, event | category | flops | bytes accessed | tf_op | source)
XLA Modules:
  0.0 647.2 jit_solution(1636274768500696253)
XLA Ops:
  35.3 7.2 %collective-permute-done.1.refs_0_ = bf16[512,1024]{1,0:T(8,128)(2,1)} collective-permute-done((bf16[512,1024]{1,0:T(8,128)(2,1)}, bf16[512,1024]{1,0:T(8,128)(2,1)}, u32[]{:S(2)}, u32[]{:S(2)}) %collective-permute-start.1) | collective-permute-done | bytes 1048608 | tf_op jit(solution)/shard_map/ppermute | solution.py:174
  48.0 16.8 %collective-permute-done.2.refs_1_ = bf16[512,1024]{1,0:T(8,128)(2,1)} collective-permute-done((bf16[512,1024]{1,0:T(8,128)(2,1)}, bf16[512,1024]{1,0:T(8,128)(2,1)}, u32[]{:S(2)}, u32[]{:S(2)}) %collective-permute-start.2) | collective-permute-done | bytes 1048608 | tf_op jit(solution)/shard_map/ppermute | solution.py:168
  68.4 24.0 %all-gather.15.cloned.1.call-done = bf16[1,1024,2048]{2,1,0:T(8,128)(2,1)} async-done(((bf16[1,256,2048]{2,1,0:T(8,128)(2,1)}), bf16[1,1024,2048]{2,1,0:T(8,128)(2,1)}) %all-gather.15.cloned.1.call-update) | async-done | bytes 4194320 | tf_op jit(solution)/shard_map/all_gather | solution.py:185
  103.5 18.0 %forward.2 = (bf16[1024,2048]{1,0:T(8,128)(2,1)}, bf16[1024,2048]{1,0:T(8,128)(2,1)}, bf16[1024,1024]{1,0:T(8,128)(2,1)}, bf16[1024,1024]{1,0:T(8,128)(2,1)}, bf...) custom-call(s32[5]{0:T(128)S(1)} %stack.55.at_ref, bf16[1024,2048]{1,0:T(8,128)(2,1)} %copy-done.4, ...), custom_call_target="tpu_custom_call" | custom-call | flops 207000 | bytes 1 | tf_op jit(solution)/shard_map/forward/pallas_call | solution.py:84
  123.0 20.3 %forward.3 = (bf16[1024,2048]{1,0:T(8,128)(2,1)}, bf16[1024,2048]{1,0:T(8,128)(2,1)}, bf16[1024,1024]{1,0:T(8,128)(2,1)}, bf16[1024,1024]{1,0:T(8,128)(2,1)}, bf...) custom-call(s32[5]{0:T(128)S(1)} %stack.55.at_ref, bf16[256,2048]{1,0:T(8,128)(2,1)S(1)} %collective-permute-done.4.refs_0_, ...), custom_call_target="tpu_custom_call" | custom-call | flops 207000 | bytes 1 | tf_op jit(solution)/shard_map/forward/pallas_call | solution.py:84
  150.9 10.6 %branch.2 = (bf16[1024,2048]{1,0:T(8,128)(2,1)}, f32[8,128]{1,0:T(8,128)S(1)}) custom-call(s32[5]{0:T(128)S(1)} %stack.55.at_ref, bf16[1024,1024]{1,0:T(8,128)(2,1)S(1)} %copy-done.9, bf16[1024,256]{1,0:T(8,128)(2,1)S(1)} %get-tuple-element.226.refs_1_.refs_7_, bf16[1024,8192]{1,0:T(8,128)(2,1)} %refs_2_.7, bf16[1024,2048]{1,0:T(8,128)(2,1)} %refs_3_.9, ...), custom_call_target="tpu_custom_call" | custom-call | flops 115000 | bytes 1 | tf_op jit(solution)/shard_map/branch/pallas_call | solution.py:84
  161.6 10.4 %branch.3 = (bf16[1024,2048]{1,0:T(8,128)(2,1)}, f32[8,128]{1,0:T(8,128)S(1)}) custom-call(s32[5]{0:T(128)S(1)} %stack.55.at_ref, bf16[1024,1024]{1,0:T(8,128)(2,1)S(1)} %copy-done.8, bf16[1024,256]{1,0:T(8,128)(2,1)S(1)} %get-tuple-element.222.refs_1_.refs_6_, bf16[1024,8192]{1,0:T(8,128)(2,1)} %refs_2_.7, bf16[1024,2048]{1,0:T(8,128)(2,1)} %refs_3_.9, ...), custom_call_target="tpu_custom_call" | custom-call | flops 115000 | bytes 1 | tf_op jit(solution)/shard_map/branch/pallas_call | solution.py:84
  178.4 9.9 %down_back.2 = (bf16[1024,1024]{1,0:T(8,128)(2,1)S(1)}, bf16[1024,256]{1,0:T(8,128)(2,1)S(1)}, f32[8,1024]{1,0:T(8,128)S(1)}, f32[8,128]{1,0:T(8,128)S(1)}) custom-call(s32[5]{0:T(128)S(1)} %stack.55.at_ref, bf16[1024,2048]{1,0:T(8,128)(2,1)} %bitcast.82, bf16[1024,1024]{1,0:T(8,128)(2,1)} %get-tuple-element.233.refs_1_, bf16[1024,8192]{1,0:T(8,128)(2,1)} %refs_2_.7, ...), custom_call_target="tpu_custom_call" | custom-call | flops 115000 | bytes 1 | tf_op jit(solution)/shard_map/down_back/pallas_call | solution.py:84
  192.4 8.4 %grad_down.2 = (bf16[1024,512]{1,0:T(8,128)(2,1)S(1)}, bf16[1024,512]{1,0:T(8,128)(2,1)S(1)}, f32[8,128]{1,0:T(8,128)S(1)}) custom-call(s32[5]{0:T(128)S(1)} %stack.55.at_ref, bf16[1024,2048]{1,0:T(8,128)(2,1)} %bitcast.83, bf16[1024,2048]{1,0:T(8,128)(2,1)} %copy-done.64, bf16[1024,1024]{1,0:T(8,128)(2,1)} %get-tuple-element.218.refs_0_.refs_2_, ...), custom_call_target="tpu_custom_call" | custom-call | flops 103500 | bytes 1 | tf_op jit(solution)/shard_map/grad_down/pallas_call | solution.py:84
  202.1 9.2 %grad_down.3 = (f32[1024,512]{1,0:T(8,128)S(1)}, f32[1024,512]{1,0:T(8,128)}, f32[8,128]{1,0:T(8,128)S(1)}) custom-call(s32[5]{0:T(128)S(1)} %stack.55.at_ref, bf16[1024,2048]{1,0:T(8,128)(2,1)} %bitcast.84, bf16[1024,2048]{1,0:T(8,128)(2,1)} %copy-done.64, bf16[1024,1024]{1,0:T(8,128)(2,1)} %get-tuple-element.218.refs_0_.refs_2_, ...), custom_call_target="tpu_custom_call" | custom-call | flops 103500 | bytes 1 | tf_op jit(solution)/shard_map/grad_down/pallas_call | solution.py:84
  212.9 9.9 %down_back.3 = (bf16[1024,1024]{1,0:T(8,128)(2,1)S(1)}, bf16[1024,256]{1,0:T(8,128)(2,1)S(1)}, f32[8,1024]{1,0:T(8,128)S(1)}, f32[8,128]{1,0:T(8,128)S(1)}) custom-call(s32[5]{0:T(128)S(1)} %stack.55.at_ref, bf16[1024,2048]{1,0:T(8,128)(2,1)} %copy-done.64, bf16[1024,1024]{1,0:T(8,128)(2,1)} %get-tuple-element.244.refs_1_, bf16[1024,8192]{1,0:T(8,128)(2,1)} %refs_2_.7, ...), custom_call_target="tpu_custom_call" | custom-call | flops 115000 | bytes 1 | tf_op jit(solution)/shard_map/down_back/pallas_call | solution.py:84
  227.8 9.5 %grad_up.2 = (bf16[1024,1024]{1,0:T(8,128)(2,1)S(1)}, f32[1024,128]{1,0:T(8,128)S(1)}, f32[8,128]{1,0:T(8,128)S(1)}) custom-call(s32[5]{0:T(128)S(1)} %stack.55.at_ref, bf16[1024,2048]{1,0:T(8,128)(2,1)} %get-tuple-element.241.refs_0_, bf16[1024,2048]{1,0:T(8,128)(2,1)} %get-tuple-element.242.refs_1_, bf16[1024,1024]{1,0:T(8,128)(2,1)} %copy-done.5, ...), custom_call_target="tpu_custom_call" | custom-call | flops 103500 | bytes 1 | tf_op jit(solution)/shard_map/grad_up/pallas_call | solution.py:84
  259.2 10.2 %grad_up.3 = (f32[1024,1024]{1,0:T(8,128)}, f32[1024,128]{1,0:T(8,128)S(1)}, f32[8,128]{1,0:T(8,128)S(1)}) custom-call(s32[5]{0:T(128)S(1)} %stack.55.at_ref, bf16[1024,2048]{1,0:T(8,128)(2,1)} %get-tuple-element.241.refs_0_, bf16[1024,2048]{1,0:T(8,128)(2,1)} %get-tuple-element.242.refs_1_, bf16[1024,1024]{1,0:T(8,128)(2,1)S(1)} %copy-done.6, ...), custom_call_target="tpu_custom_call" | custom-call | flops 103500 | bytes 1 | tf_op jit(solution)/shard_map/grad_up/pallas_call | solution.py:84
  282.0 10.6 %grad_att.2 = (f32[1024,1024]{1,0:T(8,128)}, f32[1024,128]{1,0:T(8,128)S(1)}, f32[8,128]{1,0:T(8,128)S(1)}) custom-call(s32[5]{0:T(128)S(1)} %stack.55.at_ref, bf16[1024,2048]{1,0:T(8,128)(2,1)} %get-tuple-element.272.refs_0_, bf16[1024,2048]{1,0:T(8,128)(2,1)} %get-tuple-element.273.refs_1_, bf16[1024,768]{1,0:T(8,128)(2,1)S(1)} %copy-done.10, ...), custom_call_target="tpu_custom_call" | custom-call | flops 103500 | bytes 1 | tf_op jit(solution)/shard_map/grad_att/pallas_call | solution.py:84
  306.0 9.9 %grad_att.3 = (bf16[1024,1024]{1,0:T(8,128)(2,1)}, f32[1024,128]{1,0:T(8,128)S(1)}, f32[8,128]{1,0:T(8,128)S(1)}) custom-call(s32[5]{0:T(128)S(1)} %stack.55.at_ref, bf16[1024,2048]{1,0:T(8,128)(2,1)} %get-tuple-element.272.refs_0_, bf16[1024,2048]{1,0:T(8,128)(2,1)} %get-tuple-element.273.refs_1_, bf16[1024,768]{1,0:T(8,128)(2,1)S(1)} %copy-done.10, ...), custom_call_target="tpu_custom_call" | custom-call | flops 103500 | bytes 1 | tf_op jit(solution)/shard_map/grad_att/pallas_call | solution.py:84
  328.3 13.0 %back.2 = (bf16[1024,2048]{1,0:T(8,128)(2,1)}, f32[8,128]{1,0:T(8,128)S(1)}) custom-call(s32[5]{0:T(128)S(1)} %stack.55.at_ref, bf16[1024,768]{1,0:T(8,128)(2,1)S(1)} %copy-done.11, bf16[1024,1024]{1,0:T(8,128)(2,1)} %copy-done.7, f32[8,2048]{1,0:T(8,128)S(1)} %get-tuple-element.210.refs_1_.refs_4_.refs_2_, bf16[1024,2048]{1,0:T(8,128)(2,1)} %refs_3_.11, ...), custom_call_target="tpu_custom_call" | custom-call | flops 149500 | bytes 1 | tf_op jit(solution)/shard_map/back/pallas_call | solution.py:84
  341.3 6.7 %all-gather.21.cloned.1.call-done = bf16[2048,512]{1,0:T(8,128)(2,1)} async-done(((bf16[512,512]{1,0:T(8,128)(2,1)}), bf16[2048,512]{1,0:T(8,128)(2,1)}) %all-gather.21.cloned.1.call-update) | async-done | bytes 2097168 | tf_op jit(solution)/shard_map/all_gather | solution.py:739
  373.8 13.3 %back.3 = (bf16[1024,2048]{1,0:T(8,128)(2,1)}, f32[8,128]{1,0:T(8,128)S(1)}) custom-call(s32[5]{0:T(128)S(1)} %stack.55.at_ref, bf16[1024,768]{1,0:T(8,128)(2,1)S(1)} %copy-done.10, bf16[1024,1024]{1,0:T(8,128)(2,1)} %copy-done.5, f32[8,2048]{1,0:T(8,128)S(1)} %get-tuple-element.210.refs_1_.refs_4_.refs_2_, bf16[1024,2048]{1,0:T(8,128)(2,1)} %refs_3_.11, ...), custom_call_target="tpu_custom_call" | custom-call | flops 149500 | bytes 1 | tf_op jit(solution)/shard_map/back/pallas_call | solution.py:84
  387.1 16.0 %collective-permute-done.23.refs_1_ = bf16[1024,1024]{1,0:T(8,128)(2,1)S(1)} collective-permute-done((bf16[1024,1024]{1,0:T(8,128)(2,1)}, bf16[1024,1024]{1,0:T(8,128)(2,1)S(1)}, u32[]{:S(2)}, u32[]{:S(2)}) %collective-permute-start.23) | collective-permute-done | bytes 2097184 | tf_op jit(solution)/shard_map/ppermute | solution.py:174
  413.9 15.9 %collective-permute-done.28.refs_1_ = f32[180,128]{1,0:T(8,128)S(1)} collective-permute-done((f32[180,128]{1,0:T(8,128)S(1)}, f32[180,128]{1,0:T(8,128)S(1)}, u32[]{:S(2)}, u32[]{:S(2)}) %collective-permute-start.28) | collective-permute-done | bytes 92192 | tf_op jit(solution)/shard_map/ppermute | solution.py:168
  472.4 63.2 %collective-permute-done.31.refs_0_ = bf16[4,512,1024]{2,1,0:T(8,128)(2,1)} collective-permute-done((bf16[4,512,1024]{2,1,0:T(8,128)(2,1)}, bf16[4,512,1024]{2,1,0:T(8,128)(2,1)}, u32[]{:S(2)}, u32[]{:S(2)}) %collective-permute-start.31) | collective-permute-done | bytes 4194336 | tf_op jit(solution)/shard_map/ppermute | solution.py:168
  554.6 6.6 %place.30 = (f32[1024,8192]{1,0:T(8,128)}, f32[8,128]{1,0:T(8,128)S(1)}) custom-call(s32[5]{0:T(128)S(1)} %stack.55.at_ref, bf16[4,1,512,1024]{3,2,1,0:T(8,128)(2,1)} %bitcast.47.refs_0_, f32[1024,8192]{1,0:T(8,128)} %get-tuple-element.345.refs_1_, f32[8,128]{1,0:T(8,128)S(1)} %get-tuple-element.351.refs_2_), custom_call_target="tpu_custom_call", output_to_operand_aliasing={{0}: (2, {})} | custom-call | flops 46000 | bytes 1 | tf_op jit(solution)/shard_map/place/pallas_call | solution.py:84
  583.9 23.8 %collective-permute-done.32.refs_0_ = bf16[4,512,768]{2,1,0:T(8,128)(2,1)S(1)} collective-permute-done((bf16[4,512,768]{2,1,0:T(8,128)(2,1)}, bf16[4,512,768]{2,1,0:T(8,128)(2,1)S(1)}, u32[]{:S(2)}, u32[]{:S(2)}) %collective-permute-start.32) | collective-permute-done | bytes 3145760 | tf_op jit(solution)/shard_map/ppermute | solution.py:168
  613.1 14.2 %reduce-scatter.5.cloned.1.call-done.refs_2_ = bf16[256,2048]{1,0:T(8,128)(2,1)} async-done(((bf16[1024,2048]{1,0:T(8,128)(2,1)}), bf16[256,2048]{1,0:T(8,128)(2,1)}) %reduce-scatter.5.cloned.1.call-update) | async-done | bytes 1048592 | tf_op jit(solution)/shard_map/reduce_scatter | solution.py:477
  (387 shorter events, 274.2 us)
Async XLA Ops:
  7.2 85.3 %all-gather.15.cloned.1.call-start = ((), (), s32[]{:S(2)}) async-start(), calls=%async_computation.4 | async-start | bytes 5242880 | tf_op jit(solution)/shard_map/all_gather | solution.py:185
  7.9 169.9 %all-gather.17.cloned.1.call-start = ((), (), s32[]{:S(2)}) async-start(), calls=%async_computation.5 | async-start | bytes 5242880 | tf_op jit(solution)/shard_map/all_gather | solution.py:186
  22.3 80.0 %collective-permute-start.3 = (bf16[1024,768]{1,0:T(8,128)(2,1)}, bf16[1024,768]{1,0:T(8,128)(2,1)S(1)}, u32[]{:S(2)}, u32[]{:S(2)}) collective-permute-start(bf16[1024,768]{1,0:T(8,128)(2,1)} %pad_maximum_fusion.1), channel_id=1, source_target_pairs={{0,1},{1,0},{2,3},{3,2},{4,5},{5,4},{6,7},{7,6},{8,9},{9,8},{10,11... | collective-permute-start | bytes 4718600 | tf_op jit(solution)/shard_map/ppermute | solution.py:174
  47.1 103.8 %collective-permute-start.8 = (bf16[1024,1280]{1,0:T(8,128)(2,1)}, bf16[1024,1280]{1,0:T(8,128)(2,1)}, u32[]{:S(2)}, u32[]{:S(2)}) collective-permute-start(bf16[1024,1280]{1,0:T(8,128)(2,1)} %pad_maximum_fusion), channel_id=1, source_target_pairs={{0,1},{1,0},{2,3},{3,2},{4,5},{5,4},{6,7},{7,6},{8,9},{9,8},{10,11... | collective-permute-start | bytes 7864328 | tf_op jit(solution)/shard_map/ppermute | solution.py:174
  47.4 230.0 %reduce-scatter.3.cloned.1.call-start = ((), (), s32[]{:S(2)}) async-start(), calls=%async_computation.2 | async-start | bytes 5242880 | tf_op jit(solution)/shard_map/reduce_scatter | solution.py:477
  177.8 123.4 %all-gather.19.cloned.1.call-start = ((), (), s32[]{:S(2)}) async-start(), calls=%async_computation.6 | async-start | bytes 2621440 | tf_op jit(solution)/shard_map/all_gather | solution.py:739
  240.9 107.0 %all-gather.21.cloned.1.call-start = ((), (), s32[]{:S(2)}) async-start(), calls=%async_computation.7 | async-start | bytes 2621440 | tf_op jit(solution)/shard_map/all_gather | solution.py:739
  241.2 51.4 %collective-permute-start.15 = (bf16[1024,1024]{1,0:T(8,128)(2,1)}, bf16[1024,1024]{1,0:T(8,128)(2,1)}, u32[]{:S(2)}, u32[]{:S(2)}) collective-permute-start(bf16[1024,1024]{1,0:T(8,128)(2,1)} %copy-done.62), channel_id=1, source_target_pairs={{0,16},{8,24},{16,0},{24,8},{1,17},{9,25},{17,1},{25,9},{2,18},{10... | collective-permute-start | bytes 6291464 | tf_op jit(solution)/shard_map/ppermute | solution.py:168
  242.4 27.0 %collective-permute-start.11 = (bf16[1024,512]{1,0:T(8,128)(2,1)}, bf16[1024,512]{1,0:T(8,128)(2,1)}, u32[]{:S(2)}, u32[]{:S(2)}) collective-permute-start(bf16[1024,512]{1,0:T(8,128)(2,1)} %copy-done.39), channel_id=1, source_target_pairs={{0,1},{1,0},{2,3},{3,2},{4,5},{5,4},{6,7},{7,6},{8,9},{9,8},{10,11... | collective-permute-start | bytes 3145736 | tf_op jit(solution)/shard_map/ppermute | solution.py:174
  273.3 25.1 %collective-permute-start.14 = (bf16[512,512]{1,0:T(8,128)(2,1)}, bf16[512,512]{1,0:T(8,128)(2,1)}, u32[]{:S(2)}, u32[]{:S(2)}) collective-permute-start(bf16[512,512]{1,0:T(8,128)(2,1)} %get-tuple-element.269), channel_id=1, source_target_pairs={{0,16},{8,24},{16,0},{24,8},{1,17},{9,25},{17,1},{25,9},{2,18},{10... | collective-permute-start | bytes 1572872 | tf_op jit(solution)/shard_map/ppermute | solution.py:168
  300.8 139.2 %all-gather.23.cloned.1.call-start = ((), (), s32[]{:S(2)}) async-start(), calls=%async_computation.8 | async-start | bytes 5242880 | tf_op jit(solution)/shard_map/all_gather | solution.py:739
  304.0 47.5 %collective-permute-start.16 = (bf16[4,512,512]{2,1,0:T(8,128)(2,1)}, bf16[4,512,512]{2,1,0:T(8,128)(2,1)}, u32[]{:S(2)}, u32[]{:S(2)}) collective-permute-start(bf16[4,512,512]{2,1,0:T(8,128)(2,1)} %get-tuple-element.281), channel_id=1, source_target_pairs={{0,16},{8,24},{16,0},{24,8},{1,17},{9,25},{17,1},{25,9},{2,18},{10... | collective-permute-start | bytes 6291464 | tf_op jit(solution)/shard_map/ppermute | solution.py:168
  316.4 35.6 %collective-permute-start.20 = (bf16[512,1024]{1,0:T(8,128)(2,1)}, bf16[512,1024]{1,0:T(8,128)(2,1)}, u32[]{:S(2)}, u32[]{:S(2)}) collective-permute-start(bf16[512,1024]{1,0:T(8,128)(2,1)} %copy-done.63), channel_id=1, source_target_pairs={{0,1},{1,0},{2,3},{3,2},{4,5},{5,4},{6,7},{7,6},{8,9},{9,8},{10,11... | collective-permute-start | bytes 3145736 | tf_op jit(solution)/shard_map/ppermute | solution.py:174
  354.9 182.6 %all-gather.25.cloned.1.call-start = ((), (), s32[]{:S(2)}) async-start(), calls=%async_computation.9 | async-start | bytes 3932160 | tf_op jit(solution)/shard_map/all_gather | solution.py:739
  356.0 47.1 %collective-permute-start.23 = (bf16[1024,1024]{1,0:T(8,128)(2,1)}, bf16[1024,1024]{1,0:T(8,128)(2,1)S(1)}, u32[]{:S(2)}, u32[]{:S(2)}) collective-permute-start(bf16[1024,1024]{1,0:T(8,128)(2,1)} %get-tuple-element.312), channel_id=1, source_target_pairs={{0,1},{1,0},{2,3},{3,2},{4,5},{5,4},{6,7},{7,6},{8,9},{9,8},{10,11... | collective-permute-start | bytes 6291464 | tf_op jit(solution)/shard_map/ppermute | solution.py:174
  357.2 49.4 %collective-permute-start.22 = (bf16[4,512,512]{2,1,0:T(8,128)(2,1)}, bf16[4,512,512]{2,1,0:T(8,128)(2,1)S(1)}, u32[]{:S(2)}, u32[]{:S(2)}) collective-permute-start(bf16[4,512,512]{2,1,0:T(8,128)(2,1)} %copy-done.17), channel_id=1, source_target_pairs={{0,16},{8,24},{16,0},{24,8},{1,17},{9,25},{17,1},{25,9},{2,18},{10... | collective-permute-start | bytes 6291464 | tf_op jit(solution)/shard_map/ppermute | solution.py:168
  404.1 26.2 %collective-permute-start.25 = (bf16[512,1024]{1,0:T(8,128)(2,1)S(1)}, bf16[512,1024]{1,0:T(8,128)(2,1)S(1)}, u32[]{:S(2)}, u32[]{:S(2)}) collective-permute-start(bf16[512,1024]{1,0:T(8,128)(2,1)S(1)} %get-tuple-element.319), channel_id=1, source_target_pairs={{0,16},{8,24},{16,0},{24,8},{1,17},{9,25},{17,1},{25,9},{2,18},{10... | collective-permute-start | bytes 3145736 | tf_op jit(solution)/shard_map/ppermute | solution.py:168
  432.6 135.7 %all-gather.27.cloned.1.call-start = ((), (), s32[]{:S(2)}) async-start(), calls=%async_computation.10 | async-start | bytes 2621440 | tf_op jit(solution)/shard_map/all_gather | solution.py:739
  443.6 92.0 %collective-permute-start.31 = (bf16[4,512,1024]{2,1,0:T(8,128)(2,1)}, bf16[4,512,1024]{2,1,0:T(8,128)(2,1)}, u32[]{:S(2)}, u32[]{:S(2)}) collective-permute-start(bf16[4,512,1024]{2,1,0:T(8,128)(2,1)} %get-tuple-element.330), channel_id=1, source_target_pairs={{0,16},{8,24},{16,0},{24,8},{1,17},{9,25},{17,1},{25,9},{2,18},{10... | collective-permute-start | bytes 12582920 | tf_op jit(solution)/shard_map/ppermute | solution.py:168
  445.5 181.8 %reduce-scatter.5.cloned.1.call-start = ((), (), s32[]{:S(2)}) async-start(), calls=%async_computation.3 | async-start | bytes 5242880 | tf_op jit(solution)/shard_map/reduce_scatter | solution.py:477
  536.1 25.1 %collective-permute-start.34 = (bf16[4,512,1024]{2,1,0:T(8,128)(2,1)}, bf16[4,512,1024]{2,1,0:T(8,128)(2,1)}, u32[]{:S(2)}, u32[]{:S(2)}) collective-permute-start(bf16[4,512,1024]{2,1,0:T(8,128)(2,1)} %get-tuple-element.344), channel_id=1, source_target_pairs={{0,8},{8,0},{16,24},{24,16},{1,9},{9,1},{17,25},{25,17},{2,10},{10... | collective-permute-start | bytes 12582920 | tf_op jit(solution)/shard_map/ppermute | solution.py:165
  538.2 69.6 %collective-permute-start.32 = (bf16[4,512,768]{2,1,0:T(8,128)(2,1)}, bf16[4,512,768]{2,1,0:T(8,128)(2,1)S(1)}, u32[]{:S(2)}, u32[]{:S(2)}) collective-permute-start(bf16[4,512,768]{2,1,0:T(8,128)(2,1)} %get-tuple-element.342), channel_id=1, source_target_pairs={{0,16},{8,24},{16,0},{24,8},{1,17},{9,25},{17,1},{25,9},{2,18},{10... | collective-permute-start | bytes 9437192 | tf_op jit(solution)/shard_map/ppermute | solution.py:168
  539.4 28.4 %collective-permute-start.33 = (f32[180,128]{1,0:T(8,128)S(1)}, f32[180,128]{1,0:T(8,128)S(1)}, u32[]{:S(2)}, u32[]{:S(2)}) collective-permute-start(f32[180,128]{1,0:T(8,128)S(1)} %get-tuple-element.343.refs_0_), channel_id=1, source_target_pairs={{0,2},{2,0},{4,6},{6,4},{1,3},{3,1},{5,7},{7,5},{8,10},{10,8},{12,... | collective-permute-start | bytes 276488 | tf_op jit(solution)/shard_map/ppermute | solution.py:921
  608.3 26.1 %collective-permute-start.38 = (bf16[4,512,768]{2,1,0:T(8,128)(2,1)S(1)}, bf16[4,512,768]{2,1,0:T(8,128)(2,1)}, u32[]{:S(2)}, u32[]{:S(2)}) collective-permute-start(bf16[4,512,768]{2,1,0:T(8,128)(2,1)S(1)} %get-tuple-element.365), channel_id=1, source_target_pairs={{0,8},{8,0},{16,24},{24,16},{1,9},{9,1},{17,25},{25,17},{2,10},{10... | collective-permute-start | bytes 9437192 | tf_op jit(solution)/shard_map/ppermute | solution.py:165
  (100 other events, 987.9 us)
Sparse Core Ops, SparseCore 0:
  9.6 82.8 all-gather.14
  94.0 79.2 all-gather.16
  177.9 75.3 reduce-scatter.2
  254.8 46.4 all-gather.18
  303.3 44.6 all-gather.20
  355.0 79.7 all-gather.22
  437.1 61.9 all-gather.24
  500.8 44.0 all-gather.26
  547.2 80.0 reduce-scatter.4
